TPU v7x, 32 devices: a whole 2x2x4 slice. The times are simulated.
32 devices in a mesh: context: 4 (over z), seq: 4 (over y, x), tensor: 2 (over core).
Axes of the slice: x: 2, y: 2, z: 4, core: 2. Of those that a mesh axis runs over, the one named last changes fastest.
Arguments:
- queries: bfloat16 [4096, 2048], P(('seq', 'context'), 'tensor'), parts along dimension 0, may hold values from -9 to 9
- key_states: bfloat16 [4096, 512], P(('seq', 'context'), 'tensor'), parts along dimension 0, may hold values from -4 to 4
- value_states: bfloat16 [4096, 512], P(('seq', 'context'), 'tensor'), parts along dimension 0, may hold values from -6 to 6
- segment_ids: int32 [4096], P('seq'), parts along dimension 0, may hold values from 0 to 3, never falling along the last dimension, each value on 1 to 768 neighbouring positions
- hidden: bfloat16 [4096, 2048], P(('seq', 'context')), parts along dimension 0, may hold values from -6 to 6
- attn_out_weight: bfloat16 [2048, 2048], P('tensor'), may hold values from -0.125 to 0.125
- norm_gain: bfloat16 [2048], replicated, may hold values from 0.5 to 1.5
- gate_weight: bfloat16 [2048, 4096], P(None, 'tensor'), may hold values from -0.125 to 0.125
- inner_weight: bfloat16 [2048, 4096], P(None, 'tensor'), may hold values from -0.125 to 0.125
- state_proj_weight: bfloat16 [2048, 256], replicated, may hold values from -0.125 to 0.125
- step_weight: bfloat16 [2048, 64], P(None, 'tensor'), may hold values from -0.125 to 0.125
- conv_inner: bfloat16 [4, 4096], P(None, 'tensor'), may hold values from -3 to 3
- conv_state: bfloat16 [4, 256], replicated, may hold values from -3 to 3
- step_bias: float32 [64], P('tensor'), may hold values from -4 to 0
- decay_log: float32 [64], P('tensor'), may hold values from -12 to 3
- skip_gain: float32 [64], P('tensor'), may hold values from 0.5 to 1.5
- out_gain: bfloat16 [4096], P('tensor'), may hold values from 0.5 to 1.5
Outputs:
- residual: bfloat16 [4096, 2048], P(('seq', 'context')), parts along dimension 0
- mixed: bfloat16 [4096, 4096], P(('seq', 'context'), 'tensor'), parts along dimension 0
There are 4 independent parts, one for each index of `seq`. A program takes and returns all parts, laid end to end along the dimension named above; an argument that names none is the same for every part. Nothing has to cross between parts.
Inputs may be any that keep to these rules, and one draw needn't show every extreme that they name: `segment_ids`: segment ids never fall along a sequence.
All inputs are finite; a program needn't handle non-finite values.
Results may differ from a plain program's by a relative error of at most 0.012.
Values may be sent and summed in bfloat16 or wider, within the bound.
A program may use at most 128 MiB of HBM per device.

v0:
```python
import jax
import jax.numpy as jnp
from jax import lax
from jax.sharding import PartitionSpec as P

ATT_HEADS = 16
KV_HEADS = 4
HEAD_DIM = 128
STATE = 128
CONV = 4
WINDOW = 2048
D_INNER = 4096


EPSILON = 1e-05


def passed_along(x, axis, by):
    length = lax.axis_size(axis)
    pairs = [(i, i + by) for i in range(length) if 0 <= i + by < length]
    return lax.ppermute(x, axis, pairs)


def prefix(x, axis, combine, identity):
    length, position = (lax.axis_size(axis), lax.axis_index(axis))
    everything = jax.tree.map(
        lambda part, kind: lax.all_gather(part.astype(kind), axis), x, (jnp.bfloat16, jnp.bfloat16)
    )
    start = jax.tree.map(
        lambda part, zero: jnp.broadcast_to(jnp.asarray(zero, part.dtype), part.shape), x, identity
    )

    def step(k, before):
        reached = k < position
        new = combine(
            before, jax.tree.map(lambda part, own: part[k].astype(own.dtype), everything, x)
        )
        return jax.tree.map(lambda a, b: jnp.where(reached, a, b), new, before)

    return lax.fori_loop(0, length, step, start)


def attend(query_rows, key_rows, value_rows, query_pos, key_pos, query_seg, key_seg):
    groups = ATT_HEADS // KV_HEADS
    count = query_rows.shape[0]
    local_heads = key_rows.shape[1] // HEAD_DIM
    shaped_q = query_rows.reshape(count, local_heads, groups, HEAD_DIM)
    shaped_k = key_rows.reshape(-1, local_heads, HEAD_DIM)
    shaped_v = value_rows.reshape(-1, local_heads, HEAD_DIM)
    scores = jnp.einsum(
        "tgjd,sgd->gjts", shaped_q, shaped_k, preferred_element_type=jnp.float32
    ) * HEAD_DIM ** (-0.5)
    allowed = (key_pos[None, :] <= query_pos[:, None]) & (
        query_pos[:, None] - key_pos[None, :] < WINDOW
    )
    allowed = allowed & (key_seg[None, :] == query_seg[:, None])
    scores = jnp.where(allowed, scores, -jnp.inf)
    highest = jnp.max(scores, axis=-1, keepdims=True)
    weights = jnp.exp(scores - highest)
    probs = (weights / jnp.sum(weights, axis=-1, keepdims=True)).astype(jnp.bfloat16)
    blended = jnp.einsum("gjts,sgd->tgjd", probs, shaped_v, preferred_element_type=jnp.float32)
    return blended.astype(jnp.bfloat16).reshape(count, -1)


def causal_conv(raw_rows, taps, seg_rows):
    count = raw_rows.shape[0] - CONV + 1
    target = seg_rows[CONV - 1 :]
    total = jnp.zeros((count, raw_rows.shape[1]), jnp.float32)
    for tap in range(CONV):
        keep = (seg_rows[tap : tap + count] == target).astype(jnp.float32)
        total = (
            total
            + taps[tap].astype(jnp.float32)[None, :]
            * raw_rows[tap : tap + count].astype(jnp.float32)
            * keep[:, None]
        )
    return jax.nn.silu(total).astype(jnp.bfloat16)


def local_terms(shaped, read_in, read_out, step, rate, seg_rows):
    count = shaped.shape[0]
    running = jnp.cumsum(rate, axis=0)
    order = jnp.arange(count, dtype=jnp.int32)
    same = (seg_rows[:, None] == seg_rows[None, :]) & (order[:, None] >= order[None, :])
    gap = running.T[:, :, None] - running.T[:, None, :]
    decay = jnp.where(same[None], jnp.exp(jnp.where(same[None], gap, 0.0)), 0.0)
    pairwise = jnp.einsum("tn,sn->ts", read_out, read_in, preferred_element_type=jnp.float32)
    mixing = (decay * pairwise[None] * step.T[:, None, :]).astype(jnp.bfloat16)
    within = jnp.einsum("hts,shp->thp", mixing, shaped, preferred_element_type=jnp.float32)
    tail = (
        jnp.exp(running[-1][None, :] - running)
        * (seg_rows == seg_rows[-1]).astype(jnp.float32)[:, None]
    )
    weighted = ((tail * step)[:, :, None] * shaped.astype(jnp.float32)).astype(jnp.bfloat16)
    end_state = jnp.einsum("thp,tn->hpn", weighted, read_in, preferred_element_type=jnp.float32)
    return (within, running, end_state)


def per_device(
    queries,
    key_states,
    value_states,
    segment_ids,
    hidden,
    attn_out_weight,
    norm_gain,
    gate_weight,
    inner_weight,
    state_proj_weight,
    step_weight,
    conv_inner,
    conv_state,
    step_bias,
    decay_log,
    skip_gain,
    out_gain,
):
    row_count = hidden.shape[0]
    device_index = lax.axis_index("context")
    anchor = device_index * row_count
    reach = min(WINDOW // row_count, lax.axis_size("context") - 1)
    margin = reach * row_count
    seg_padded = jnp.concatenate([jnp.full((margin,), -1, jnp.int32), segment_ids])
    key_seg = lax.dynamic_slice_in_dim(seg_padded, anchor, margin + row_count, 0)
    query_seg = lax.dynamic_slice_in_dim(segment_ids, anchor, row_count, 0)
    query_pos = anchor + jnp.arange(row_count, dtype=jnp.int32)
    key_pos = anchor - margin + jnp.arange(margin + row_count, dtype=jnp.int32)
    key_parts = []
    value_parts = []
    for offset in range(reach, 0, -1):
        moved_keys, moved_values = passed_along((key_states, value_states), "context", offset)
        key_parts.append(moved_keys)
        value_parts.append(moved_values)
    near_keys = jnp.concatenate(key_parts + [key_states])
    near_values = jnp.concatenate(value_parts + [value_states])
    attended = attend(queries, near_keys, near_values, query_pos, key_pos, query_seg, key_seg)
    partial_out = jnp.dot(attended, attn_out_weight, preferred_element_type=jnp.float32)
    projected = lax.psum(partial_out, "tensor")
    residual = (hidden.astype(jnp.float32) + projected).astype(jnp.bfloat16)
    wide = residual.astype(jnp.float32)
    normed = (
        wide
        * lax.rsqrt(jnp.mean(wide * wide, axis=-1, keepdims=True) + EPSILON)
        * norm_gain.astype(jnp.float32)[None, :]
    ).astype(jnp.bfloat16)
    gate = jnp.dot(normed, gate_weight, preferred_element_type=jnp.float32).astype(jnp.bfloat16)
    inner_raw = jnp.dot(normed, inner_weight, preferred_element_type=jnp.float32).astype(
        jnp.bfloat16
    )
    state_raw = jnp.dot(normed, state_proj_weight, preferred_element_type=jnp.float32).astype(
        jnp.bfloat16
    )
    step_raw = jnp.dot(normed, step_weight, preferred_element_type=jnp.float32)
    step = jax.nn.softplus(step_raw + step_bias[None, :])
    rate = -jnp.exp(decay_log)[None, :] * step
    rim_inner, rim_state = passed_along(
        (inner_raw[row_count - CONV + 1 :], state_raw[row_count - CONV + 1 :]), "context", 1
    )
    conv_seg = lax.dynamic_slice_in_dim(
        jnp.concatenate([jnp.full((CONV - 1,), -1, jnp.int32), segment_ids]),
        anchor,
        row_count + CONV - 1,
        0,
    )
    inner = causal_conv(jnp.concatenate([rim_inner, inner_raw]), conv_inner, conv_seg)
    state_conv = causal_conv(jnp.concatenate([rim_state, state_raw]), conv_state, conv_seg)
    read_in = state_conv[:, :STATE]
    read_out = state_conv[:, STATE:]
    local_heads = step_weight.shape[1]
    shaped = inner.reshape(row_count, local_heads, -1)
    within, running, end_state = local_terms(shaped, read_in, read_out, step, rate, query_seg)
    prior_seg = conv_seg[CONV - 2]
    end_decay = jnp.exp(running[-1]) * (query_seg[-1] == prior_seg).astype(jnp.float32)

    def combine(earlier, later):
        return (earlier[0] * later[0], later[0][:, None, None] * earlier[1] + later[1])

    identity = (jnp.ones_like(end_decay), jnp.zeros_like(end_state))
    _, incoming_state = prefix((end_decay, end_state), "context", combine, identity)
    entry = jnp.exp(running) * (query_seg == prior_seg).astype(jnp.float32)[:, None]
    carried = (
        jnp.einsum(
            "tn,hpn->thp",
            read_out,
            incoming_state.astype(jnp.bfloat16),
            preferred_element_type=jnp.float32,
        )
        * entry[:, :, None]
    )
    ssm_out = within + carried + skip_gain[None, :, None] * shaped.astype(jnp.float32)
    gated = ssm_out.reshape(row_count, -1) * jax.nn.silu(gate.astype(jnp.float32))
    squares = lax.psum(jnp.sum(gated * gated, axis=-1), "tensor")
    mixed = (
        gated
        * lax.rsqrt(squares / D_INNER + EPSILON)[:, None]
        * out_gain.astype(jnp.float32)[None, :]
    ).astype(jnp.bfloat16)
    return (residual, mixed)


def solution(mesh):
    in_specs = (
        P(("seq", "context"), "tensor"),
        P(("seq", "context"), "tensor"),
        P(("seq", "context"), "tensor"),
        P("seq"),
        P(("seq", "context"), None),
        P("tensor", None),
        P(),
        P(None, "tensor"),
        P(None, "tensor"),
        P(),
        P(None, "tensor"),
        P(None, "tensor"),
        P(),
        P("tensor"),
        P("tensor"),
        P("tensor"),
        P("tensor"),
    )
    out_specs = (P(("seq", "context"), None), P(("seq", "context"), "tensor"))
    return jax.shard_map(
        per_device, mesh=mesh, in_specs=in_specs, out_specs=out_specs, check_vma=False
    )
```

profile of v0, /device:TPU:0, one launch (start us, length us, event | category | flops | bytes accessed | tf_op | source)
XLA Modules:
  0.0 173.7 jit_solution(3680788515201315477)
XLA Ops:
  7.2 0.0 all-reduce.4.cloned.1.call-start
  7.2 1.1 copy.40
  8.3 7.0 %collective-permute-start.3 = (bf16[256,256]{0,1:T(8,128)(2,1)S(1)}, bf16[256,256]{0,1:T(8,128)(2,1)S(1)}, u32[]{:S(2)}, u32[]{:S(2)}) collective-permute-start(bf16[256,256]{0,1:T(8,128)(2,1)S(1)} %copy.40), channel_id=1, source_target_pairs={{0,24},{1,25},{2,26},{3,27},{4,28},{5,29},{6,30},{7,31}} | collective-permute-start | bytes 393224 | tf_op jit(solution)/shard_map/ppermute | solution.py:21
  15.3 1.3 collective-permute-start.4
  16.6 2.5 %collective-permute-start.5 = (bf16[256,256]{0,1:T(8,128)(2,1)S(1)}, bf16[256,256]{0,1:T(8,128)(2,1)S(1)}, u32[]{:S(2)}, u32[]{:S(2)}) collective-permute-start(bf16[256,256]{0,1:T(8,128)(2,1)S(1)} %copy.40), channel_id=1, source_target_pairs={{0,8},{8,16},{16,24},{1,9},{9,17},{17,25},{2,10},{10,18},{18,26},{... | collective-permute-start | bytes 393224 | tf_op jit(solution)/shard_map/ppermute | solution.py:21
  19.1 1.3 collective-permute-start
  20.4 1.3 collective-permute-start.1
  21.7 0.8 pad_dynamic-slice_fusion
  22.5 0.6 slice.115
  23.0 1.3 compare_convert_fusion
  24.4 0.8 pad_dynamic-slice_fusion.1
  25.1 2.7 %collective-permute-done = bf16[256,256]{1,0:T(8,128)(2,1)S(1)} collective-permute-done((bf16[256,256]{1,0:T(8,128)(2,1)}, bf16[256,256]{1,0:T(8,128)(2,1)S(1)}, u32[]{:S(2)}, u32[]{:S(2)}) %collective-permute-start) | collective-permute-done | bytes 131104 | tf_op jit(solution)/shard_map/ppermute | solution.py:21
  27.8 1.3 collective-permute-start.2
  29.1 0.8 fusion.29
  29.9 1.4 reshape.140
  31.3 1.0 collective-permute-done.2
  32.2 0.9 pad_maximum_fusion.1
  33.2 0.2 copy.39
  33.4 0.1 pad_maximum_fusion.2
  33.5 6.0 %fusion.65 = (f32[2,4,256]{2,1,0:T(4,128)S(1)}, f32[2,4,256,1024]{2,3,1,0:T(8,128)}) fusion(pred[256,1024]{0,1:T(8,128)(4,1)S(1)} %fusion.29, bf16[1024,2,128,1]{0,2,3,1:T(8,128)(2,1)S(1)} %bitcast.115, bf16[256,2,4,128]{3,2,1,0:T(4,128)(2,1)S(1)} %reshape.140), kind=kOutput, calls=%fused_computation.121 | convolution fusion | flops 545260544 | bytes 9707520 | tf_op jit(solution)/shard_map/sub | solution.py:59
  39.5 4.3 %fusion.23 = bf16[2,128,4,256]{3,1,2,0:T(8,128)(2,1)S(1)} fusion(bf16[1024,2,128,1]{0,2,3,1:T(8,128)(2,1)S(1)} %bitcast.114, f32[2,4,256,1024]{2,3,1,0:T(8,128)} %get-tuple-element.147, f32[2,4,256]{2,1,0:T(4,128)S(1)} %get-tuple-element.146), kind=kOutput, calls=%fused_computation.44 | convolution fusion | flops 541327360 | bytes 9445376 | tf_op jit(solution)/shard_map/gjts,sgd->tgjd/dot_general | solution.py:61
  43.7 0.3 copy-done.17
  44.0 2.6 %fusion.70 = f32[256,2048]{1,0:T(8,128)} fusion(bf16[256,1024]{0,1:T(8,128)(2,1)S(1)} %bitcast.127, bf16[1024,2048]{1,0:T(8,128)(2,1)S(1)} %copy-done.17), kind=kOutput, calls=%fused_computation.122 | convolution fusion | flops 1073741824 | bytes 6815744 | tf_op jit(solution)/shard_map/dot_general | solution.py:137
  46.6 0.0 all-reduce.4.cloned.1.call-update
  46.7 0.0 all-gather.4.cloned.1.call-start
  46.7 0.7 slice.114
  47.4 0.7 compare_convert_fusion.1
  48.1 0.1 compare_convert_fusion.4
  48.2 26.3 %all-reduce.4.cloned.1.call-done = f32[256,2048]{1,0:T(8,128)} async-done(((f32[256,2048]{1,0:T(8,128)}), f32[256,2048]{1,0:T(8,128)}) %all-reduce.4.cloned.1.call-update) | async-done | bytes 2097168 | tf_op jit(solution)/shard_map/psum | solution.py:138
  74.5 2.0 %fusion.14 = (f32[256]{0:T(256)S(1)}, bf16[256,2048]{1,0:T(8,128)(2,1)S(1)}) fusion(f32[256,2048]{1,0:T(8,128)} %all-reduce.4.cloned.1.call-done, bf16[256,2048]{1,0:T(8,128)(2,1)S(1)} %copy-done.1), kind=kLoop, calls=%fused_computation.28 | loop fusion | flops 3145472 | bytes 4195328 | tf_op jit(solution)/shard_map/reduce_sum | solution.py:143
  76.6 0.5 convolution_convert_fusion.3
  77.1 3.7 %collective-permute-start.7 = (bf16[3,256]{1,0:T(4,128)(2,1)S(1)}, bf16[3,256]{1,0:T(4,128)(2,1)S(1)}, u32[]{:S(2)}, u32[]{:S(2)}) collective-permute-start(bf16[3,256]{1,0:T(4,128)(2,1)S(1)} %slice.122), channel_id=1, source_target_pairs={{0,8},{8,16},{16,24},{1,9},{9,17},{17,25},{2,10},{10,18},{18,26},{... | collective-permute-start | bytes 4616 | tf_op jit(solution)/shard_map/ppermute | solution.py:21
  80.8 0.5 convolution_add_fusion
  81.2 0.6 compare_select_fusion.1
  81.9 0.6 reduce-window.6
  82.4 0.2 slice_reduce_fusion
  82.6 0.7 copy_bitcast_fusion
  83.3 0.2 slice_reduce_fusion.1
  83.5 5.8 %convolution_convert_fusion.1 = bf16[256,2048]{1,0:T(8,128)(2,1)S(1)} fusion(bf16[2048,2048]{1,0:T(8,128)(2,1)} %param.27, bf16[256,2048]{1,0:T(8,128)(2,1)S(1)} %get-tuple-element.128, f32[2048]{0:T(1024)S(1)} %convert_element_type.163, f32[256]{0:T(256)S(1)} %add_rsqrt_fusion.1), kind=kOutput, calls=%fused_computation.27 | convolution fusion | flops 2150105088 | bytes 10494976 | tf_op jit(solution)/shard_map/dot_general | solution.py:147
  89.3 3.4 %collective-permute-start.6 = (bf16[3,2048]{1,0:T(4,128)(2,1)S(1)}, bf16[3,2048]{1,0:T(4,128)(2,1)S(1)}, u32[]{:S(2)}, u32[]{:S(2)}) collective-permute-start(bf16[3,2048]{1,0:T(4,128)(2,1)S(1)} %slice.116), channel_id=1, source_target_pairs={{0,8},{8,16},{16,24},{1,9},{9,17},{17,25},{2,10},{10,18},{18,26},{... | collective-permute-start | bytes 36872 | tf_op jit(solution)/shard_map/ppermute | solution.py:21
  92.7 0.7 exponential_multiply_fusion
  93.4 0.2 multiply_convert_fusion.6
  93.6 0.5 collective-permute-done.6
  94.2 1.9 %multiply_convert_fusion.3 = bf16[256,2048]{1,0:T(8,128)(2,1)S(1)} fusion(bf16[256,2048]{1,0:T(8,128)(2,1)S(1)} %convolution_convert_fusion.1, bf16[3,2048]{1,0:T(4,128)(2,1)S(1)} %collective-permute-done.6, f32[2048]{0:T(1024)S(1)} %bitcast.119, f32[256]{0:T(256)S(1)} %get-tuple-element.144, f32[2048]{0:T(1024)S(1)} %bitcast.120, ...), kind=kLoop, calls=%fused_computation.40 | loop fusion | flops 14680064 | bytes 2145280 | tf_op jit(solution)/shard_map/convert_element_type | solution.py:77
  96.1 0.5 copy.47
  96.7 1.3 convolution_convert_fusion.2
  97.9 0.0 all-gather.4.cloned.1.call-update
  99.2 0.7 fusion.41
  99.9 0.2 fusion.56
  100.1 10.3 %all-gather.1 = bf16[4,1,32]{2,1,0:T(2,128)(2,1)S(1)} all-gather(bf16[1,1,32]{2,1,0:T(2,128)(2,1)S(1)} %bitcast.125), channel_id=1, replica_groups=mesh['context'=4,'seq'=4,'tensor'=2] {'context'}, dimensions={0}, use_global_device_ids=true | all-gather | bytes 320 | tf_op jit(solution)/shard_map/all_gather | solution.py:27
  110.5 0.2 fusion.47
  110.7 34.2 %all-gather.4.cloned.1.call-done = bf16[128,64,128]{2,1,0:T(8,128)(2,1)} async-done(((bf16[32,64,128]{2,1,0:T(8,128)(2,1)}), bf16[128,64,128]{2,1,0:T(8,128)(2,1)}) %all-gather.4.cloned.1.call-update) | async-done | bytes 2097168 | tf_op jit(solution)/shard_map/all_gather | solution.py:27
  144.8 5.3 %while.14 = (s32[]{:T(128)}, f32[32,64,128]{2,1,0:T(8,128)S(1)}, s32[]{:T(128)}, bf16[4,32]{1,0:T(4,128)(2,1)S(1)}, bf16[4,32,64,128]{3,2,1,0:T(8,128)(2,1)}, /*index=5*/s32[]{:T(128)}, s32[]{:T(128)}) while((s32[]{:T(128)}, f32[32,64,128]{2,1,0:T(8,128)S(1)}, s32[]{:T(128)}, bf16[4,32]{1,0:T(4,128)(2,1)S(1)}, ...), condition=%wide.region_7.8_spmd.clone, body=%wide.region_6.7_spmd.clone.sunk | while | flops 1310756 | bytes 2621865 | solution.py:40
  144.8 1.3 fusion.82
  146.2 1.3 fusion.82
  147.5 1.3 fusion.82
  148.8 1.3 fusion.82
  150.2 0.4 fusion.32
  150.7 0.7 copy-done.4
  151.4 2.8 %fusion.18 = f32[256,32,64]{0,2,1:T(8,128)S(1)} fusion(bf16[256,32,64]{0,2,1:T(8,128)(2,1)S(1)} %bitcast.113, f32[256,32,64]{0,2,1:T(8,128)S(1)} %fusion.32, f32[32,256]{1,0:T(8,128)S(1)} %copy-done.7, f32[256,256]{1,0:T(8,128)S(1)} %fusion.47, f32[32,256]{1,0:T(8,128)S(1)} %copy-done.8, pred[256,256]{1,0:T(8,128)(4,1)S(1)} %copy-done.5, ...), kind=kOutput, calls=%fused_computation.32 | convolution fusion | flops 283639808 | bytes 5668992 | tf_op jit(solution)/shard_map/hts,shp->thp/dot_general | solution.py:89
  154.3 1.8 %copy.50 = f32[256,2048]{1,0:T(8,128)} copy(f32[256,2048]{0,1:T(8,128)S(1)} %bitcast.111) | data formatting | bytes 4194304 | tf_op jit(solution)/shard_map/reshape | solution.py:191
  156.1 7.0 %multiply_reduce_fusion = (f32[256]{0:T(256)S(1)}, f32[256,2048]{1,0:T(8,128)S(1)}) fusion(f32[256,2048]{1,0:T(8,128)} %copy.50, bf16[2048,2048]{1,0:T(8,128)(2,1)} %param.26, bf16[256,2048]{1,0:T(8,128)(2,1)} %copy-done.2, f32[2048]{0:T(1024)S(1)} %copy-done.11, f32[256]{0:T(256)S(1)} %copy-done.16), kind=kOutput, calls=%fused_computation.39 | convolution fusion | flops 2154299136 | bytes 13641728 | tf_op jit(solution)/shard_map/dot_general | solution.py:146
  163.2 2.5 %psum.15 = f32[256]{0:T(256)S(1)} all-reduce(f32[256]{0:T(256)S(1)} %get-tuple-element.148), channel_id=1, replica_groups=mesh['context'=4,'seq'=4,'tensor'=2] {'tensor'}, use_global_device_ids=true, to_apply=%region_9.10 | all-reduce | flops 256 | bytes 2048 | tf_op jit(solution)/shard_map/psum | solution.py:192
  165.6 1.2 multiply_convert_fusion.2
  (66 shorter events, 0.3 us)
Async XLA Ops:
  7.2 69.4 %copy-start = (bf16[2048,256]{1,0:T(8,128)(2,1)S(1)}, bf16[2048,256]{1,0:T(8,128)(2,1)}, u32[]{:S(2)}) copy-start(bf16[2048,256]{1,0:T(8,128)(2,1)} %param.28) | copy-start | bytes 3145732
  7.2 67.3 %all-reduce.4.cloned.1.call-start = ((), (), s32[]{:S(2)}) async-start(), calls=%async_computation | async-start | bytes 4194304 | tf_op jit(solution)/shard_map/psum | solution.py:138
  8.3 25.1 %collective-permute-start.3 = (bf16[256,256]{0,1:T(8,128)(2,1)S(1)}, bf16[256,256]{0,1:T(8,128)(2,1)S(1)}, u32[]{:S(2)}, u32[]{:S(2)}) collective-permute-start(bf16[256,256]{0,1:T(8,128)(2,1)S(1)} %copy.40), channel_id=1, source_target_pairs={{0,24},{1,25},{2,26},{3,27},{4,28},{5,29},{6,30},{7,31}} | collective-permute-start | bytes 393224 | tf_op jit(solution)/shard_map/ppermute | solution.py:21
  15.3 18.1 %collective-permute-start.4 = (bf16[256,256]{0,1:T(8,128)(2,1)S(1)}, bf16[256,256]{0,1:T(8,128)(2,1)S(1)}, u32[]{:S(2)}, u32[]{:S(2)}) collective-permute-start(bf16[256,256]{0,1:T(8,128)(2,1)S(1)} %copy.40), channel_id=1, source_target_pairs={{0,16},{8,24},{1,17},{9,25},{2,18},{10,26},{3,19},{11,27},{4,20},{... | collective-permute-start | bytes 393224 | tf_op jit(solution)/shard_map/ppermute | solution.py:21
  16.6 16.8 %collective-permute-start.5 = (bf16[256,256]{0,1:T(8,128)(2,1)S(1)}, bf16[256,256]{0,1:T(8,128)(2,1)S(1)}, u32[]{:S(2)}, u32[]{:S(2)}) collective-permute-start(bf16[256,256]{0,1:T(8,128)(2,1)S(1)} %copy.40), channel_id=1, source_target_pairs={{0,8},{8,16},{16,24},{1,9},{9,17},{17,25},{2,10},{10,18},{18,26},{... | collective-permute-start | bytes 393224 | tf_op jit(solution)/shard_map/ppermute | solution.py:21
  19.1 8.7 %collective-permute-start = (bf16[256,256]{1,0:T(8,128)(2,1)}, bf16[256,256]{1,0:T(8,128)(2,1)S(1)}, u32[]{:S(2)}, u32[]{:S(2)}) collective-permute-start(bf16[256,256]{1,0:T(8,128)(2,1)} %param.21), channel_id=1, source_target_pairs={{0,24},{1,25},{2,26},{3,27},{4,28},{5,29},{6,30},{7,31}} | collective-permute-start | bytes 393224 | tf_op jit(solution)/shard_map/ppermute | solution.py:21
  20.4 10.9 %collective-permute-start.1 = (bf16[256,256]{1,0:T(8,128)(2,1)}, bf16[256,256]{1,0:T(8,128)(2,1)S(1)}, u32[]{:S(2)}, u32[]{:S(2)}) collective-permute-start(bf16[256,256]{1,0:T(8,128)(2,1)} %param.21), channel_id=1, source_target_pairs={{0,16},{8,24},{1,17},{9,25},{2,18},{10,26},{3,19},{11,27},{4,20},{... | collective-permute-start | bytes 393224 | tf_op jit(solution)/shard_map/ppermute | solution.py:21
  27.8 4.5 %collective-permute-start.2 = (bf16[256,256]{1,0:T(8,128)(2,1)}, bf16[256,256]{1,0:T(8,128)(2,1)S(1)}, u32[]{:S(2)}, u32[]{:S(2)}) collective-permute-start(bf16[256,256]{1,0:T(8,128)(2,1)} %param.21), channel_id=1, source_target_pairs={{0,8},{8,16},{16,24},{1,9},{9,17},{17,25},{2,10},{10,18},{18,26},{... | collective-permute-start | bytes 393224 | tf_op jit(solution)/shard_map/ppermute | solution.py:21
  39.5 4.6 %copy-start.17 = (bf16[1024,2048]{1,0:T(8,128)(2,1)S(1)}, bf16[1024,2048]{1,0:T(8,128)(2,1)}, u32[]{:S(2)}) copy-start(bf16[1024,2048]{1,0:T(8,128)(2,1)} %param.24) | copy-start | bytes 12582916
  46.6 0.8 copy-start.13
  46.6 0.8 copy-start.19
  46.6 1.6 copy-start.12
  46.6 1.6 copy-start.6
  46.6 27.9 %copy-start.1 = (bf16[256,2048]{1,0:T(8,128)(2,1)S(1)}, bf16[256,2048]{1,0:T(8,128)(2,1)}, u32[]{:S(2)}) copy-start(bf16[256,2048]{1,0:T(8,128)(2,1)} %param.23) | copy-start | bytes 3145732
  46.7 98.2 %all-gather.4.cloned.1.call-start = ((), (), s32[]{:S(2)}) async-start(), calls=%async_computation.1 | async-start | bytes 2621440 | tf_op jit(solution)/shard_map/all_gather | solution.py:27
  47.4 36.1 %copy-start.10 = (f32[2048]{0:T(1024)}, f32[2048]{0:T(1024)S(1)}, u32[]{:S(2)}) copy-start(f32[2048]{0:T(1024)S(1)} %convert_element_type.163) | copy-start | bytes 24580
  76.5 7.0 %copy-start.2 = (bf16[256,2048]{1,0:T(8,128)(2,1)}, bf16[256,2048]{1,0:T(8,128)(2,1)S(1)}, u32[]{:S(2)}) copy-start(bf16[256,2048]{1,0:T(8,128)(2,1)S(1)} %get-tuple-element.128) | copy-start | bytes 3145732
  76.5 4.2 %copy-start.18 = (bf16[2048,32]{0,1:T(8,128)(2,1)S(1)}, bf16[2048,32]{0,1:T(8,128)(2,1)}, u32[]{:S(2)}) copy-start(bf16[2048,32]{0,1:T(8,128)(2,1)} %param.29) | copy-start | bytes 393220
  76.5 4.2 %copy-start.20 = (f32[32]{0:T(128)S(1)}, f32[32]{0:T(128)}, u32[]{:S(2)}) copy-start(f32[32]{0:T(128)} %param.32) | copy-start | bytes 388
  76.5 7.0 %copy-start.15 = (f32[256]{0:T(256)}, f32[256]{0:T(256)S(1)}, u32[]{:S(2)}) copy-start(f32[256]{0:T(256)S(1)} %add_rsqrt_fusion.1) | copy-start | bytes 3076
  77.1 16.4 %collective-permute-start.7 = (bf16[3,256]{1,0:T(4,128)(2,1)S(1)}, bf16[3,256]{1,0:T(4,128)(2,1)S(1)}, u32[]{:S(2)}, u32[]{:S(2)}) collective-permute-start(bf16[3,256]{1,0:T(4,128)(2,1)S(1)} %slice.122), channel_id=1, source_target_pairs={{0,8},{8,16},{16,24},{1,9},{9,17},{17,25},{2,10},{10,18},{18,26},{... | collective-permute-start | bytes 4616 | tf_op jit(solution)/shard_map/ppermute | solution.py:21
  89.3 4.8 %collective-permute-start.6 = (bf16[3,2048]{1,0:T(4,128)(2,1)S(1)}, bf16[3,2048]{1,0:T(4,128)(2,1)S(1)}, u32[]{:S(2)}, u32[]{:S(2)}) collective-permute-start(bf16[3,2048]{1,0:T(4,128)(2,1)S(1)} %slice.116), channel_id=1, source_target_pairs={{0,8},{8,16},{16,24},{1,9},{9,17},{17,25},{2,10},{10,18},{18,26},{... | collective-permute-start | bytes 36872 | tf_op jit(solution)/shard_map/ppermute | solution.py:21
  96.1 3.1 %copy-start.14 = (bf16[2048]{0:T(1024)(128)(2,1)S(1)}, bf16[2048]{0:T(1024)(128)(2,1)}, u32[]{:S(2)}) copy-start(bf16[2048]{0:T(1024)(128)(2,1)} %param.35) | copy-start | bytes 12292
  96.6 48.2 %copy-start.3 = (bf16[256,2048]{0,1:T(8,128)(2,1)}, bf16[256,2048]{0,1:T(8,128)(2,1)S(1)}, u32[]{:S(2)}) copy-start(bf16[256,2048]{0,1:T(8,128)(2,1)S(1)} %copy.47) | copy-start | bytes 3145732
  150.2 1.2 copy-start.4
  150.2 1.2 copy-start.5
  150.2 1.2 copy-start.7
  150.2 1.2 copy-start.8
  150.2 1.2 copy-start.9
  150.2 1.2 copy-start.21
  154.2 1.9 %copy-start.11 = (f32[2048]{0:T(1024)S(1)}, f32[2048]{0:T(1024)}, u32[]{:S(2)}) copy-start(f32[2048]{0:T(1024)} %copy-done.10) | copy-start | bytes 24580
  154.3 1.9 %copy-start.16 = (f32[256]{0:T(256)S(1)}, f32[256]{0:T(256)}, u32[]{:S(2)}) copy-start(f32[256]{0:T(256)} %copy-done.15) | copy-start | bytes 3076
Sparse Core Ops, SparseCore 0:
  46.8 27.6 all-reduce.3
  98.1 46.7 all-gather.3
where the time goes:
time: 174 us
  waiting for transfers between devices  64.6 us (37%)
  matrix products  31.3 us (18%)
  starting transfers between devices  21.7 us (12%)
  other arithmetic  18.8 us (11%)
  between operations  15.8 us (9%)
  blocking collectives  12.8 us (7%)
  local copies, waits for them, and re-layouts  8.56 us (5%)
    all_gather x1, waiting for transfers between devices, prefix(): lax.all_gather(part.astype(kind), axis)  34.2 us
    psum x1, waiting for transfers between devices, per_device(): projected = lax.psum(partial_out, 'tensor')  26.3 us
    ppermute x8, starting transfers between devices, passed_along(): return lax.ppermute(x, axis, pairs)  21.7 us
    all_gather x1, blocking collectives, prefix(): lax.all_gather(part.astype(kind), axis)  10.3 us
    dot_general x1, matrix products, per_device(): jnp.dot(normed, gate_weight, preferred_element_type=jnp.float32)  7.04 us
    sub x1, matrix products, attend(): weights = jnp.exp(scores - highest)  5.96 us
    dot_general x1, matrix products, per_device(): jnp.dot(normed, inner_weight, preferred_element_type=jnp.float32)  5.76 us
    select_n x4, other arithmetic, step(): return jax.tree.map(lambda a, b: jnp.where(reached, a, b), new, before)  5.19 us
  transfers between devices with their start and end apart: 10, of which 5 were waited for; matrix products, arithmetic and copies ran while one was open for 11% of the time, Pallas kernels for 0%

commit v1 on v0

v1 whole, which is shorter than its diff:
```python
import functools

import jax
import jax.numpy as jnp
from jax import lax
from jax.experimental import pallas as pl
from jax.experimental.pallas import tpu as pltpu
from jax.sharding import PartitionSpec as P

ATT_HEADS = 16
KV_HEADS = 4
HEAD_DIM = 128
STATE = 128
CONV = 4
WINDOW = 2048
EPSILON = 1e-05
LANES = 128
HALO = 16
PAD = 8
LOW = -1e30
F32 = jnp.float32
BF16 = jnp.bfloat16


def dot(a, b):
    return jnp.dot(a, b, preferred_element_type=F32)


def silu(x):
    return x / (1.0 + jnp.exp(-x))


def wide(x, width):
    return jnp.concatenate([x] * (width // LANES), axis=1)


def split(x, parts):
    out = []
    for _ in range(parts):
        piece = x.astype(BF16)
        out.append(piece)
        x = x - piece.astype(F32)
    return out


def body(
    cfg,
    q_hbm, k_hbm, v_hbm, seg_ref, hid_hbm, wo_hbm, gain_ref, wg_hbm, wi_hbm, ws_hbm, wt_ref,
    ci_ref, cs_ref, bias_ref, decay_ref, skip_ref, og_ref,
    res_hbm, mix_hbm,
    q, kbuf, vbuf, hid, wo, wg, wi, ws, att, m_s, l_s, acc, mask, res, normed,
    raw, sraw, halo_out, halo_in, segc, keep, step, run, runT, stepT, gate, inner, rin, rinT, rout,
    pm, state, carry_in, carry_out, within, gated, sq, sq_in,
    local_sem, ksend, krecv, vsend, vrecv, wsend, wrecv, asend, arecv, hsend, hrecv,
    csend, crecv, ssend, srecv,
):
    C, TP, reach = cfg["context"], cfg["tensor"], cfg["reach"]
    T, D = hid.shape
    DI = wi.shape[1]
    SH = wt_ref.shape[1]
    PH = DI // SH
    heads = q.shape[1] // HEAD_DIM
    groups = ATT_HEADS // KV_HEADS
    NC, _, W = carry_in.shape
    i = lax.axis_index("context")
    core = lax.axis_index("tensor")
    has_next = i + 1 < C
    has_prev = i > 0
    partners = [lax.rem(core + k, TP) for k in range(1, TP)]

    def remote(src, dst, s, r, **where):
        return pltpu.make_async_remote_copy(
            src_ref=src, dst_ref=dst, send_sem=s, recv_sem=r,
            device_id=where, device_id_type=pl.DeviceIdType.MESH,
        )

    barrier = pltpu.get_barrier_semaphore()

    def greet(**where):
        pl.semaphore_signal(
            barrier, inc=1, device_id=where, device_id_type=pl.DeviceIdType.MESH
        )

    @pl.when(has_next)
    def _():
        greet(context=i + 1)

    @pl.when(has_prev)
    def _():
        greet(context=i - 1)

    for partner in partners:
        greet(tensor=partner)

    locals_ = [
        pltpu.make_async_copy(src, dst, local_sem.at[n])
        for n, (src, dst) in enumerate(
            [(q_hbm, q), (k_hbm, kbuf.at[0]), (v_hbm, vbuf.at[0]), (wo_hbm, wo.at[core]),
             (hid_hbm, hid), (ws_hbm, ws), (wi_hbm, wi), (wg_hbm, wg)]
        )
    ]
    for copy in locals_[:3]:
        copy.start()

    pl.semaphore_wait(
        barrier, has_next.astype(jnp.int32) + has_prev.astype(jnp.int32) + TP - 1
    )

    def hop(d):
        to = i + 1
        return (
            remote(kbuf.at[d], kbuf.at[d + 1], ksend.at[d], krecv.at[d], context=to),
            remote(vbuf.at[d], vbuf.at[d + 1], vsend.at[d], vrecv.at[d], context=to),
        )

    locals_[1].wait()
    locals_[2].wait()
    if reach > 0:
        @pl.when(has_next)
        def _():
            for copy in hop(0):
                copy.start()

    for copy in locals_[3:]:
        copy.start()
    wcopies = [
        remote(wo_hbm, wo.at[core], wsend.at[n], wrecv.at[n], tensor=partner)
        for n, partner in enumerate(partners)
    ]
    for copy in wcopies:
        copy.start()

    rows = lax.broadcasted_iota(jnp.int32, (T, T), 0)
    cols = lax.broadcasted_iota(jnp.int32, (T, T), 1)

    def seg_row(block):
        return seg_ref[:, pl.ds(pl.multiple_of(block * T, LANES), T)].astype(F32)

    def column(row):
        return jnp.sum(jnp.where(rows == cols, row, 0.0), axis=1, keepdims=True)

    own_row = seg_row(i)
    own_col = column(own_row)
    prev_col = jnp.where(has_prev, column(seg_row(jnp.maximum(i - 1, 0))), -1.0)
    segc[PAD:, :] = jnp.broadcast_to(own_col, (T, LANES))
    segc[:PAD, :] = jnp.broadcast_to(prev_col[T - PAD :, :], (PAD, LANES))
    for tap in range(CONV):
        keep[tap] = (segc[pl.ds(PAD - CONV + 1 + tap, T), :] == segc[PAD:, :]).astype(F32)

    m_s[...] = jnp.full(m_s.shape, LOW, F32)
    l_s[...] = jnp.zeros(l_s.shape, F32)
    acc[...] = jnp.zeros(acc.shape, F32)
    scale = HEAD_DIM ** (-0.5)

    def attend(d):
        gap = d * T + rows - cols
        key_row = seg_row(i - d)
        allowed = (gap >= 0) & (gap < WINDOW) & (segc[PAD:, :1] == key_row)
        mask[...] = jnp.where(allowed, 0.0, LOW)

        def one(h, carry):
            at = pl.multiple_of(h * HEAD_DIM, HEAD_DIM)
            kat = pl.multiple_of((h // groups) * HEAD_DIM, HEAD_DIM)
            s = lax.dot_general(
                q[:, pl.ds(at, HEAD_DIM)], kbuf[d, :, pl.ds(kat, HEAD_DIM)],
                (((1,), (1,)), ((), ())), preferred_element_type=F32,
            )
            s = s * scale + mask[...]
            old = m_s[h]
            new = jnp.maximum(old, jnp.max(s, axis=1, keepdims=True))
            alpha = jnp.exp(old - new)
            p = jnp.exp(s - wide(new, T))
            m_s[h] = new
            l_s[h] = l_s[h] * alpha + jnp.sum(p, axis=1, keepdims=True)
            acc[h] = acc[h] * alpha + dot(p.astype(BF16), vbuf[d, :, pl.ds(kat, HEAD_DIM)])
            return carry

        lax.fori_loop(0, heads, one, 0, unroll=2)

    locals_[0].wait()
    attend(0)

    if reach > 0:
        def arrive(d, carry):
            @pl.when(i >= d)
            def _():
                for copy in hop(d - 1):
                    copy.wait_recv()

                @pl.when(has_next & (d < reach))
                def _():
                    for copy in hop(d):
                        copy.start()

                attend(d)

            return carry

        lax.fori_loop(1, reach + 1, arrive, 0)

    def finish(h, carry):
        at = pl.multiple_of(h * HEAD_DIM, HEAD_DIM)
        att[core, :, pl.ds(at, HEAD_DIM)] = (acc[h] / l_s[h]).astype(BF16)
        return carry

    lax.fori_loop(0, heads, finish, 0, unroll=2)
    acopies = [
        remote(att.at[core], att.at[core], asend.at[n], arecv.at[n], tensor=partner)
        for n, partner in enumerate(partners)
    ]
    for copy in acopies:
        copy.start()
    locals_[3].wait()
    locals_[4].wait()
    for copy in wcopies:
        copy.wait()
    for copy in acopies:
        copy.wait()

    def project(c, squares):
        at = pl.ds(pl.multiple_of(c * W, LANES), W)
        total = dot(att[0], wo[0, :, at])
        for k in range(1, TP):
            total = total + dot(att[k], wo[k, :, at])
        r = (hid[:, at].astype(F32) + total).astype(BF16)
        res[:, at] = r
        r = r.astype(F32)
        return squares + jnp.sum(r * r, axis=1, keepdims=True)

    squares = lax.fori_loop(0, D // W, project, jnp.zeros((T, 1), F32))
    res_copy = pltpu.make_async_copy(res, res_hbm, local_sem.at[8])
    res_copy.start()
    inv = lax.rsqrt(squares / D + EPSILON)

    def norm(c, carry):
        at = pl.ds(pl.multiple_of(c * W, LANES), W)
        normed[:, at] = (res[:, at].astype(F32) * inv * gain_ref[:, at].astype(F32)).astype(BF16)
        return carry

    lax.fori_loop(0, D // W, norm, 0)

    locals_[5].wait()
    x = dot(normed[...], ws[...]).astype(BF16)
    sraw[PAD:, :] = x.astype(F32)
    halo_out[:, DI:] = x[T - HALO :, :]
    locals_[6].wait()

    def project_inner(c, carry):
        at = pl.ds(pl.multiple_of(c * W, LANES), W)
        y = dot(normed[...], wi[:, at]).astype(BF16)
        raw[PAD:, at] = y.astype(F32)
        halo_out[:, at] = y[T - HALO :, :]
        return carry

    lax.fori_loop(0, NC, project_inner, 0)
    halo = remote(halo_out, halo_in, hsend.at[0], hrecv.at[0], context=i + 1)

    @pl.when(has_next)
    def _():
        halo.start()

    raw_step = dot(normed[...], wt_ref[...]) + bias_ref[...]
    soft = jnp.maximum(raw_step, 0.0) + jnp.log1p(jnp.exp(-jnp.abs(raw_step)))
    step[...] = jnp.zeros(step.shape, F32)
    step[:, :SH] = soft
    run[...] = jnp.zeros(run.shape, F32)
    run[:, :SH] = -jnp.exp(decay_ref[...]) * soft
    causal = rows >= cols
    tri = jnp.where(causal, 1.0, 0.0).astype(BF16)
    running = sum(dot(tri, piece) for piece in split(run[...], 3))
    run[...] = running
    runT[...] = running.T
    stepT[...] = step[...].T

    locals_[7].wait()

    def project_gate(c, carry):
        at = pl.ds(pl.multiple_of(c * W, LANES), W)
        gate[:, at] = dot(normed[...], wg[:, at]).astype(BF16)
        return carry

    lax.fori_loop(0, NC, project_gate, 0)

    @pl.when(has_prev)
    def _():
        halo.wait_recv()
        raw[:PAD, :] = halo_in[:, :DI].astype(F32)[HALO - PAD :, :]
        sraw[:PAD, :] = halo_in[:, DI:].astype(F32)[HALO - PAD :, :]

    @pl.when(jnp.logical_not(has_prev))
    def _():
        raw[:PAD, :] = jnp.zeros((PAD, DI), F32)
        sraw[:PAD, :] = jnp.zeros((PAD, sraw.shape[1]), F32)

    def conv(ref, taps, at, width):
        total = jnp.zeros((T, width), F32)
        for tap in range(CONV):
            total = total + (
                taps[tap : tap + 1, at].astype(F32)
                * ref[pl.ds(PAD - CONV + 1 + tap, T), at]
                * wide(keep[tap], width)
            )
        return silu(total)

    sc = conv(sraw, cs_ref, pl.ds(0, 2 * STATE), 2 * STATE)
    rin[...] = sc[:, :STATE].astype(BF16)
    rinT[...] = sc[:, :STATE].T.astype(BF16)
    rout[...] = sc[:, STATE:].astype(BF16)
    pairwise = lax.dot_general(
        rout[...], rin[...], (((1,), (1,)), ((), ())), preferred_element_type=F32
    )
    pm[...] = jnp.where(causal & (segc[PAD:, :1] == own_row), pairwise, 0.0)

    last = run[T - 1 : T, :]
    prior = segc[PAD - 1 : PAD, :]
    tail = jnp.exp(last - run[...]) * step[...]
    tail = jnp.where(segc[PAD:, :] == segc[PAD + T - 1 : PAD + T, :], tail, 0.0)
    tail = split(tail, 2)
    entry = split(jnp.where(segc[PAD:, :] == prior, jnp.exp(run[...]), 0.0), 2)
    end = jnp.where(segc[PAD + T - 1 : PAD + T, :] == prior, jnp.exp(last), 0.0)
    end = split(jnp.broadcast_to(end, (HALO, LANES)), 3)
    gain = jnp.concatenate([skip_ref[...], jnp.zeros((1, LANES - SH), F32)], axis=1)
    gain = split(jnp.broadcast_to(gain, (HALO, LANES)), 3)
    head_row = lax.broadcasted_iota(jnp.int32, (LANES, W), 0) * PH
    head_col = lax.broadcasted_iota(jnp.int32, (LANES, W), 1)

    def expand(pieces, c):
        offset = head_col + c * W - head_row
        pick = jnp.where((offset >= 0) & (offset < PH), 1.0, 0.0).astype(BF16)
        return sum(dot(piece, pick) for piece in pieces)

    def convolve(c, carry):
        at = pl.ds(pl.multiple_of(c * W, LANES), W)
        value = conv(raw, ci_ref, at, W).astype(BF16)
        inner[:, at] = value
        weighted = (expand(tail, c) * value.astype(F32)).astype(BF16)
        state[c] = dot(rinT[...], weighted)
        return carry

    lax.fori_loop(0, NC, convolve, 0)

    def onward(c):
        return remote(carry_out.at[c], carry_in.at[c], csend.at[c], crecv.at[c], context=i + 1)

    @pl.when(jnp.logical_not(has_prev))
    def _():
        carry_in[...] = jnp.zeros(carry_in.shape, BF16)

        @pl.when(has_next)
        def _():
            for c in range(NC):
                carry_out[c] = state[c].astype(BF16)
                onward(c).start()

    lane = lax.broadcasted_iota(jnp.int32, (T, LANES), 1)
    per = LANES // PH

    def mixing(h):
        col = jnp.sum(jnp.where(lane == h, run[...], 0.0), axis=1, keepdims=True)
        decay = jnp.exp(jnp.minimum(col - runT[pl.ds(h, 1), :], 0.0))
        return (decay * pm[...] * stepT[pl.ds(h, 1), :]).astype(BF16)

    def pair(n, carry):
        at = pl.ds(pl.multiple_of(n * LANES, LANES), LANES)
        value = inner[:, at]
        total = dot(mixing(n * per), value)
        for k in range(1, per):
            total = jnp.where(lane >= k * PH, dot(mixing(n * per + k), value), total)
        within[:, at] = total
        return carry

    def chunk(c, squares):
        lax.fori_loop(c * (W // LANES), (c + 1) * (W // LANES), pair, 0)
        at = pl.ds(pl.multiple_of(c * W, LANES), W)

        @pl.when(has_prev)
        def _():
            onward(c).wait_recv()

            @pl.when(has_next)
            def _():
                moved = expand(end, c)[:1, :] * carry_in[c].astype(F32) + state[c]
                carry_out[c] = moved.astype(BF16)
                onward(c).start()

        y = within[:, at] + dot(rout[...], carry_in[c]) * expand(entry, c)
        y = y + expand(gain, c)[:1, :] * inner[:, at].astype(F32)
        y = y * silu(gate[:, at].astype(F32))
        gated[:, at] = y
        return squares + jnp.sum(y * y, axis=1, keepdims=True)

    total = lax.fori_loop(0, NC, chunk, jnp.zeros((T, 1), F32))
    sq[...] = jnp.broadcast_to(total, (T, LANES))
    scopies = [
        remote(sq, sq_in.at[n], ssend.at[n], srecv.at[n], tensor=partner)
        for n, partner in enumerate(partners)
    ]
    for copy in scopies:
        copy.start()
    for copy in scopies:
        copy.wait()
    grand = sq[...]
    for n in range(TP - 1):
        grand = grand + sq_in[n]
    factor = wide(lax.rsqrt(grand / (DI * TP) + EPSILON), W)

    def scale_out(c, carry):
        at = pl.ds(pl.multiple_of(c * W, LANES), W)
        inner[:, at] = (gated[:, at] * factor * og_ref[:, at].astype(F32)).astype(BF16)
        return carry

    lax.fori_loop(0, NC, scale_out, 0)
    mix_copy = pltpu.make_async_copy(inner, mix_hbm, local_sem.at[9])
    mix_copy.start()

    @pl.when(has_next)
    def _():
        halo.wait_send()
        for c in range(NC):
            onward(c).wait_send()
        for d in range(reach):
            @pl.when(i >= d)
            def _():
                for copy in hop(d):
                    copy.wait_send()

    res_copy.wait()
    mix_copy.wait()


def per_device(cfg, *args):
    (queries, key_states, value_states, segment_ids, hidden, attn_out_weight, norm_gain,
     gate_weight, inner_weight, state_proj_weight, step_weight, conv_inner, conv_state,
     step_bias, decay_log, skip_gain, out_gain) = args
    T, D = hidden.shape
    DI = inner_weight.shape[1]
    SN = state_proj_weight.shape[1]
    KW = key_states.shape[1]
    TP, C = cfg["tensor"], cfg["context"]
    reach = min(-(-(WINDOW - 1) // T), C - 1)
    cfg = dict(cfg, reach=reach)
    heads = queries.shape[1] // HEAD_DIM
    W = min(512, DI, D)
    NC = DI // W
    hbm = pl.BlockSpec(memory_space=pl.ANY)
    vmem = pl.BlockSpec(memory_space=pltpu.VMEM)
    hops = max(reach, 1)
    peers = max(TP - 1, 1)
    V = pltpu.VMEM
    dma = pltpu.SemaphoreType.DMA
    scratch = [
        V(queries.shape, BF16), V((reach + 1, T, KW), BF16), V((reach + 1, T, KW), BF16),
        V((T, D), BF16), V((TP,) + attn_out_weight.shape, BF16), V(gate_weight.shape, BF16),
        V(inner_weight.shape, BF16), V(state_proj_weight.shape, BF16),
        V((TP,) + queries.shape, BF16),
        V((heads, T, LANES), F32), V((heads, T, LANES), F32), V((heads, T, HEAD_DIM), F32),
        V((T, T), F32), V((T, D), BF16), V((T, D), BF16),
        V((PAD + T, DI), F32), V((PAD + T, SN), F32), V((HALO, DI + SN), BF16),
        V((HALO, DI + SN), BF16), V((PAD + T, LANES), F32), V((CONV, T, LANES), F32),
        V((T, LANES), F32), V((T, LANES), F32), V((LANES, T), F32), V((LANES, T), F32),
        V((T, DI), BF16), V((T, DI), BF16), V((T, STATE), BF16), V((STATE, T), BF16),
        V((T, STATE), BF16), V((T, T), F32), V((NC, STATE, W), F32), V((NC, STATE, W), BF16),
        V((NC, STATE, W), BF16), V((T, DI), F32), V((T, DI), F32), V((T, LANES), F32),
        V((peers, T, LANES), F32),
        dma((10,)), dma((hops,)), dma((hops,)), dma((hops,)), dma((hops,)),
        dma((peers,)), dma((peers,)), dma((peers,)), dma((peers,)), dma((1,)), dma((1,)),
        dma((NC,)), dma((NC,)), dma((peers,)), dma((peers,)),
    ]
    row = lambda x: x.reshape(1, -1)
    return pl.pallas_call(
        functools.partial(body, cfg),
        out_shape=(
            jax.ShapeDtypeStruct((T, D), BF16),
            jax.ShapeDtypeStruct((T, DI), BF16),
        ),
        in_specs=[hbm, hbm, hbm, vmem, hbm, hbm, vmem, hbm, hbm, hbm] + [vmem] * 7,
        out_specs=(hbm, hbm),
        scratch_shapes=scratch,
        compiler_params=pltpu.CompilerParams(
            collective_id=0, has_side_effects=True, vmem_limit_bytes=60 * 1024 * 1024
        ),
    )(
        queries, key_states, value_states, row(segment_ids), hidden, attn_out_weight,
        row(norm_gain), gate_weight, inner_weight, state_proj_weight, step_weight,
        conv_inner, conv_state, row(step_bias), row(decay_log), row(skip_gain), row(out_gain),
    )


def solution(mesh):
    cfg = {"context": mesh.shape["context"], "tensor": mesh.shape["tensor"]}
    both, tensor = P(("seq", "context"), "tensor"), P("tensor")
    in_specs = (
        both, both, both, P("seq"), P(("seq", "context"), None), P("tensor", None), P(),
        P(None, "tensor"), P(None, "tensor"), P(), P(None, "tensor"), P(None, "tensor"), P(),
        tensor, tensor, tensor, tensor,
    )
    return jax.shard_map(
        functools.partial(per_device, cfg), mesh=mesh, in_specs=in_specs,
        out_specs=(P(("seq", "context"), None), both), check_vma=False,
    )
```

time: 174 us -> 63 us (0.36)
  the two profiles are of different devices: /device:TPU:0 before, /device:TPU:25 now
where the time goes in v1:
time: 63 us; the launch traced here: 62.7 us
  Pallas kernels  53 us (84%)
  local copies, waits for them, and re-layouts  9.09 us (14%)
  between operations  0.64 us (1%)
    pallas_call x1, Pallas kernels, per_device(): pl.pallas_call(functools.partial(body, cfg), out_shape=(jax.ShapeDtypeStr...  53 us
    unnamed x3, local copies, waits for them, and re-layouts  6.51 us
    reshape x2, local copies, waits for them, and re-layouts, per_device(): row = lambda x: x.reshape(1, -1)  2.57 us

profile of v1, /device:TPU:25, one launch (start us, length us, event | category | flops | bytes accessed | tf_op | source)
XLA Modules:
  0.0 62.7 jit_solution(17648156746730629579)
XLA Ops:
  0.6 1.3 %reshape.23.gain_ref = bf16[1,2048]{1,0:T(2,128)(2,1)} reshape(bf16[2048]{0:T(1024)(128)(2,1)} %param.23) | data formatting | bytes 8192 | tf_op jit(solution)/shard_map/reshape | solution.py:469
  1.9 1.3 %reshape.27.og_ref = bf16[1,2048]{1,0:T(2,128)(2,1)} reshape(bf16[2048]{0:T(1024)(128)(2,1)} %param.33) | data formatting | bytes 8192 | tf_op jit(solution)/shard_map/reshape | solution.py:469
  3.2 1.9 %copy.19.wt_ref = bf16[2048,32]{1,0:T(8,128)(2,1)} copy(bf16[2048,32]{0,1:T(8,128)(2,1)} %param.27) | data formatting | bytes 262144 | tf_op args[10]
  5.1 53.0 %shard_map.176 = (bf16[256,2048]{1,0:T(8,128)(2,1)}, bf16[256,2048]{1,0:T(8,128)(2,1)}) custom-call(bf16[256,1024]{1,0:T(8,128)(2,1)} %q_hbm.1, bf16[256,256]{1,0:T(8,128)(2,1)} %k_hbm.1, bf16[256,256]{1,0:T(8,128)(2,1)} %v_hbm.1, s32[1,1024]{1,0:T(1,128)} %bitcast.4, bf16[256,2048]{1,0:T(8,128)(2,1)} %hid_hbm.1, bf16[1024,2048]{1,0:T(8,128)(2,1)} %wo_hbm.1, ...), custom_call_target="tpu_custom_call" | custom-call | tf_op jit(solution)/shard_map/pallas_call | solution.py:470
  58.1 2.3 %copy.22 = bf16[256,2048]{1,0:T(8,128)(2,1)} copy(bf16[256,2048]{1,0:T(8,128)(2,1)} %get-tuple-element.4) | data formatting | bytes 2097152
  60.4 2.3 %copy.23 = bf16[256,2048]{1,0:T(8,128)(2,1)} copy(bf16[256,2048]{1,0:T(8,128)(2,1)} %get-tuple-element.5) | data formatting | bytes 2097152

commit v2 on v1

--- a/solution.py
+++ b/solution.py
@@ -17,6 +17,7 @@
 LANES = 128
 HALO = 16
 PAD = 8
+PIECES = 4
 LOW = -1e30
 F32 = jnp.float32
 BF16 = jnp.bfloat16
@@ -27,7 +28,8 @@
 
 
 def silu(x):
-    return x / (1.0 + jnp.exp(-x))
+    half = 0.5 * x
+    return half + half * jnp.tanh(half)
 
 
 def wide(x, width):
@@ -49,15 +51,15 @@
     ci_ref, cs_ref, bias_ref, decay_ref, skip_ref, og_ref,
     res_hbm, mix_hbm,
     q, kbuf, vbuf, hid, wo, wg, wi, ws, att, m_s, l_s, acc, mask, res, normed,
-    raw, sraw, halo_out, halo_in, segc, keep, step, run, runT, stepT, gate, inner, rin, rinT, rout,
-    pm, state, carry_in, carry_out, within, gated, sq, sq_in,
+    raw, sraw, halo_out, halo_in, segc, keep, step, run, runT, stepT, inner, rin, rinT, rout,
+    pm, state, carry_in, carry_out, within, gated, sq, sq_in, part, pick, coef, gains, og, skip,
     local_sem, ksend, krecv, vsend, vrecv, wsend, wrecv, asend, arecv, hsend, hrecv,
     csend, crecv, ssend, srecv,
 ):
     C, TP, reach = cfg["context"], cfg["tensor"], cfg["reach"]
     T, D = hid.shape
     DI = wi.shape[1]
-    SH = wt_ref.shape[1]
+    SH = wt_ref.shape[0]
     PH = DI // SH
     heads = q.shape[1] // HEAD_DIM
     groups = ATT_HEADS // KV_HEADS
@@ -144,8 +146,35 @@
     prev_col = jnp.where(has_prev, column(seg_row(jnp.maximum(i - 1, 0))), -1.0)
     segc[PAD:, :] = jnp.broadcast_to(own_col, (T, LANES))
     segc[:PAD, :] = jnp.broadcast_to(prev_col[T - PAD :, :], (PAD, LANES))
-    for tap in range(CONV):
+    for tap in range(CONV - 1):
         keep[tap] = (segc[pl.ds(PAD - CONV + 1 + tap, T), :] == segc[PAD:, :]).astype(F32)
+
+    gains[...] = gain_ref[...].astype(F32)
+    og[...] = og_ref[...].astype(F32)
+
+    def row_of(ref, c):
+        per = W // LANES
+        return jnp.concatenate([ref[pl.ds(c * per + k, 1), :] for k in range(per)], axis=1)
+
+    head_row = lax.broadcasted_iota(jnp.int32, (LANES, W), 0) * PH
+    head_col = lax.broadcasted_iota(jnp.int32, (LANES, W), 1)
+
+    def make_pick(c, carry):
+        offset = head_col + c * W - head_row
+        chosen = jnp.where((offset >= 0) & (offset < PH), 1.0, 0.0).astype(BF16)
+        pick[c, :LANES, :] = chosen
+        pick[c, LANES:, :] = chosen
+        return carry
+
+    lax.fori_loop(0, NC, make_pick, 0)
+
+    def pieces(x):
+        return jnp.concatenate(split(x, 2), axis=1)
+
+    gain = jnp.concatenate([skip_ref[...], jnp.zeros((1, LANES - SH), F32)], axis=1)
+    gain = pieces(jnp.broadcast_to(gain, (HALO, LANES)))
+    for c in range(NC):
+        skip[c] = dot(gain, pick[c])
 
     m_s[...] = jnp.full(m_s.shape, LOW, F32)
     l_s[...] = jnp.zeros(l_s.shape, F32)
@@ -175,7 +204,7 @@
             acc[h] = acc[h] * alpha + dot(p.astype(BF16), vbuf[d, :, pl.ds(kat, HEAD_DIM)])
             return carry
 
-        lax.fori_loop(0, heads, one, 0, unroll=2)
+        lax.fori_loop(0, heads, one, 0, unroll=4)
 
     locals_[0].wait()
     attend(0)
@@ -211,6 +240,13 @@
     for copy in acopies:
         copy.start()
     locals_[3].wait()
+
+    def project_own(c, carry):
+        at = pl.ds(pl.multiple_of(c * W, LANES), W)
+        part[:, at] = dot(att[core], wo[core, :, at])
+        return carry
+
+    lax.fori_loop(0, D // W, project_own, 0)
     locals_[4].wait()
     for copy in wcopies:
         copy.wait()
@@ -219,9 +255,9 @@
 
     def project(c, squares):
         at = pl.ds(pl.multiple_of(c * W, LANES), W)
-        total = dot(att[0], wo[0, :, at])
-        for k in range(1, TP):
-            total = total + dot(att[k], wo[k, :, at])
+        total = part[:, at]
+        for partner in partners:
+            total = total + dot(att[partner], wo[partner, :, at])
         r = (hid[:, at].astype(F32) + total).astype(BF16)
         res[:, at] = r
         r = r.astype(F32)
@@ -234,7 +270,7 @@
 
     def norm(c, carry):
         at = pl.ds(pl.multiple_of(c * W, LANES), W)
-        normed[:, at] = (res[:, at].astype(F32) * inv * gain_ref[:, at].astype(F32)).astype(BF16)
+        normed[:, at] = (res[:, at].astype(F32) * inv * row_of(gains, c)).astype(BF16)
         return carry
 
     lax.fori_loop(0, D // W, norm, 0)
@@ -259,7 +295,9 @@
     def _():
         halo.start()
 
-    raw_step = dot(normed[...], wt_ref[...]) + bias_ref[...]
+    raw_step = lax.dot_general(
+        normed[...], wt_ref[...], (((1,), (1,)), ((), ())), preferred_element_type=F32
+    ) + bias_ref[...]
     soft = jnp.maximum(raw_step, 0.0) + jnp.log1p(jnp.exp(-jnp.abs(raw_step)))
     step[...] = jnp.zeros(step.shape, F32)
     step[:, :SH] = soft
@@ -276,7 +314,7 @@
 
     def project_gate(c, carry):
         at = pl.ds(pl.multiple_of(c * W, LANES), W)
-        gate[:, at] = dot(normed[...], wg[:, at]).astype(BF16)
+        gated[:, at] = silu(dot(normed[...], wg[:, at]).astype(BF16).astype(F32))
         return carry
 
     lax.fori_loop(0, NC, project_gate, 0)
@@ -293,8 +331,8 @@
         sraw[:PAD, :] = jnp.zeros((PAD, sraw.shape[1]), F32)
 
     def conv(ref, taps, at, width):
-        total = jnp.zeros((T, width), F32)
-        for tap in range(CONV):
+        total = taps[CONV - 1 : CONV, at].astype(F32) * ref[PAD:, at]
+        for tap in range(CONV - 1):
             total = total + (
                 taps[tap : tap + 1, at].astype(F32)
                 * ref[pl.ds(PAD - CONV + 1 + tap, T), at]
@@ -315,25 +353,21 @@
     prior = segc[PAD - 1 : PAD, :]
     tail = jnp.exp(last - run[...]) * step[...]
     tail = jnp.where(segc[PAD:, :] == segc[PAD + T - 1 : PAD + T, :], tail, 0.0)
-    tail = split(tail, 2)
-    entry = split(jnp.where(segc[PAD:, :] == prior, jnp.exp(run[...]), 0.0), 2)
+    B = T // 2
+    middle = run[B - 1 : B, :]
+    coef[:T, :] = pieces(tail)
+    coef[T : 2 * T, :] = pieces(jnp.where(segc[PAD:, :] == prior, jnp.exp(run[...]), 0.0))
+    coef[2 * T : 2 * T + B, :] = pieces(jnp.exp(middle - run[:B, :]) * step[:B, :])
+    coef[2 * T + B :, :] = pieces(jnp.exp(run[B:, :] - middle))
     end = jnp.where(segc[PAD + T - 1 : PAD + T, :] == prior, jnp.exp(last), 0.0)
-    end = split(jnp.broadcast_to(end, (HALO, LANES)), 3)
-    gain = jnp.concatenate([skip_ref[...], jnp.zeros((1, LANES - SH), F32)], axis=1)
-    gain = split(jnp.broadcast_to(gain, (HALO, LANES)), 3)
-    head_row = lax.broadcasted_iota(jnp.int32, (LANES, W), 0) * PH
-    head_col = lax.broadcasted_iota(jnp.int32, (LANES, W), 1)
-
-    def expand(pieces, c):
-        offset = head_col + c * W - head_row
-        pick = jnp.where((offset >= 0) & (offset < PH), 1.0, 0.0).astype(BF16)
-        return sum(dot(piece, pick) for piece in pieces)
+    end = pieces(jnp.broadcast_to(end, (HALO, LANES)))
+    cross = pm[B:, :B].astype(BF16)
 
     def convolve(c, carry):
         at = pl.ds(pl.multiple_of(c * W, LANES), W)
         value = conv(raw, ci_ref, at, W).astype(BF16)
         inner[:, at] = value
-        weighted = (expand(tail, c) * value.astype(F32)).astype(BF16)
+        weighted = (dot(coef[:T, :], pick[c]) * value.astype(F32)).astype(BF16)
         state[c] = dot(rinT[...], weighted)
         return carry
 
@@ -355,22 +389,30 @@
     lane = lax.broadcasted_iota(jnp.int32, (T, LANES), 1)
     per = LANES // PH
 
-    def mixing(h):
-        col = jnp.sum(jnp.where(lane == h, run[...], 0.0), axis=1, keepdims=True)
-        decay = jnp.exp(jnp.minimum(col - runT[pl.ds(h, 1), :], 0.0))
-        return (decay * pm[...] * stepT[pl.ds(h, 1), :]).astype(BF16)
-
-    def pair(n, carry):
+    def pair(n):
         at = pl.ds(pl.multiple_of(n * LANES, LANES), LANES)
-        value = inner[:, at]
-        total = dot(mixing(n * per), value)
-        for k in range(1, per):
-            total = jnp.where(lane >= k * PH, dot(mixing(n * per + k), value), total)
-        within[:, at] = total
-        return carry
+        cols_of = [
+            jnp.sum(jnp.where(lane == n * per + k, run[...], 0.0), axis=1, keepdims=True)
+            for k in range(per)
+        ]
+        for low in (0, B):
+            span = slice(low, low + B)
+            value = inner[span, at]
+            left, right = [], []
+            for k in range(per):
+                h = n * per + k
+                gap = cols_of[k][span, :] - runT[pl.ds(h, 1), :][:, span]
+                decay = jnp.exp(jnp.minimum(gap, 0.0))
+                left.append((decay * pm[span, span] * stepT[pl.ds(h, 1), :][:, span]).astype(BF16))
+                here = (lane[:B, :] >= k * PH) & (lane[:B, :] < (k + 1) * PH)
+                right.append(jnp.where(here, value.astype(F32), 0.0).astype(BF16))
+            within[span, at] = dot(
+                jnp.concatenate(left, axis=1), jnp.concatenate(right, axis=0)
+            )
 
     def chunk(c, squares):
-        lax.fori_loop(c * (W // LANES), (c + 1) * (W // LANES), pair, 0)
+        for n in range(W // LANES):
+            pair(c * (W // LANES) + n)
         at = pl.ds(pl.multiple_of(c * W, LANES), W)
 
         @pl.when(has_prev)
@@ -379,13 +421,16 @@
 
             @pl.when(has_next)
             def _():
-                moved = expand(end, c)[:1, :] * carry_in[c].astype(F32) + state[c]
+                moved = dot(end, pick[c])[:1, :] * carry_in[c].astype(F32) + state[c]
                 carry_out[c] = moved.astype(BF16)
                 onward(c).start()
 
-        y = within[:, at] + dot(rout[...], carry_in[c]) * expand(entry, c)
-        y = y + expand(gain, c)[:1, :] * inner[:, at].astype(F32)
-        y = y * silu(gate[:, at].astype(F32))
+        early = (dot(coef[2 * T : 2 * T + B, :], pick[c]) * inner[:B, at].astype(F32)).astype(BF16)
+        later = dot(cross, early) * dot(coef[2 * T + B :, :], pick[c])
+        within[B:, at] = within[B:, at] + later
+        y = within[:, at] + dot(rout[...], carry_in[c]) * dot(coef[T : 2 * T, :], pick[c])
+        y = y + skip[c, :1, :] * inner[:, at].astype(F32)
+        y = y * gated[:, at]
         gated[:, at] = y
         return squares + jnp.sum(y * y, axis=1, keepdims=True)
 
@@ -406,7 +451,7 @@
 
     def scale_out(c, carry):
         at = pl.ds(pl.multiple_of(c * W, LANES), W)
-        inner[:, at] = (gated[:, at] * factor * og_ref[:, at].astype(F32)).astype(BF16)
+        inner[:, at] = (gated[:, at] * factor * row_of(og, c)).astype(BF16)
         return carry
 
     lax.fori_loop(0, NC, scale_out, 0)
@@ -426,6 +471,19 @@
 
     res_copy.wait()
     mix_copy.wait()
+
+
+def hand_out(res_in, mix_in, res_out, mix_out, sems):
+    copies = []
+    for n, (src, dst) in enumerate(((res_in, res_out), (mix_in, mix_out))):
+        size = src.shape[0] // PIECES
+        for k in range(PIECES):
+            at = pl.ds(k * size, size)
+            copies.append(pltpu.make_async_copy(src.at[at], dst.at[at], sems.at[n * PIECES + k]))
+    for copy in copies:
+        copy.start()
+    for copy in copies:
+        copy.wait()
 
 
 def per_device(cfg, *args):
@@ -456,18 +514,21 @@
         V((heads, T, LANES), F32), V((heads, T, LANES), F32), V((heads, T, HEAD_DIM), F32),
         V((T, T), F32), V((T, D), BF16), V((T, D), BF16),
         V((PAD + T, DI), F32), V((PAD + T, SN), F32), V((HALO, DI + SN), BF16),
-        V((HALO, DI + SN), BF16), V((PAD + T, LANES), F32), V((CONV, T, LANES), F32),
+        V((HALO, DI + SN), BF16), V((PAD + T, LANES), F32), V((CONV - 1, T, LANES), F32),
         V((T, LANES), F32), V((T, LANES), F32), V((LANES, T), F32), V((LANES, T), F32),
-        V((T, DI), BF16), V((T, DI), BF16), V((T, STATE), BF16), V((STATE, T), BF16),
+        V((T, DI), BF16), V((T, STATE), BF16), V((STATE, T), BF16),
         V((T, STATE), BF16), V((T, T), F32), V((NC, STATE, W), F32), V((NC, STATE, W), BF16),
         V((NC, STATE, W), BF16), V((T, DI), F32), V((T, DI), F32), V((T, LANES), F32),
-        V((peers, T, LANES), F32),
+        V((peers, T, LANES), F32), V((T, D), F32), V((NC, 2 * LANES, W), BF16),
+        V((3 * T, 2 * LANES), BF16), V((D // LANES, LANES), F32), V((DI // LANES, LANES), F32),
+        V((NC, HALO, W), F32),
         dma((10,)), dma((hops,)), dma((hops,)), dma((hops,)), dma((hops,)),
         dma((peers,)), dma((peers,)), dma((peers,)), dma((peers,)), dma((1,)), dma((1,)),
         dma((NC,)), dma((NC,)), dma((peers,)), dma((peers,)),
     ]
     row = lambda x: x.reshape(1, -1)
-    return pl.pallas_call(
+    lanes = lambda x: x.reshape(-1, LANES)
+    results = pl.pallas_call(
         functools.partial(body, cfg),
         out_shape=(
             jax.ShapeDtypeStruct((T, D), BF16),
@@ -481,9 +542,17 @@
         ),
     )(
         queries, key_states, value_states, row(segment_ids), hidden, attn_out_weight,
-        row(norm_gain), gate_weight, inner_weight, state_proj_weight, step_weight,
-        conv_inner, conv_state, row(step_bias), row(decay_log), row(skip_gain), row(out_gain),
+        lanes(norm_gain), gate_weight, inner_weight, state_proj_weight, step_weight.T,
+        conv_inner, conv_state, row(step_bias), row(decay_log), row(skip_gain), lanes(out_gain),
     )
+    return pl.pallas_call(
+        hand_out,
+        out_shape=tuple(jax.ShapeDtypeStruct(x.shape, x.dtype) for x in results),
+        in_specs=[hbm, hbm],
+        out_specs=(hbm, hbm),
+        scratch_shapes=[dma((2 * PIECES,))],
+        compiler_params=pltpu.CompilerParams(vmem_limit_bytes=60 * 1024 * 1024),
+    )(*results)
 
 
 def solution(mesh):

time: 63 us -> 115 us (1.83)
  Pallas kernels: 53 us -> 114 us
  local copies, waits for them, and re-layouts: 9.09 us -> 0 us
    pallas_call x0 -> x1, Pallas kernels: none -> 64.7 us  [per_device(): pl.pallas_call(hand_out, out_shape=tuple((jax.ShapeDtypeStruct(x.shape, x...]
    unnamed x3 -> x0, local copies, waits for them, and re-layouts: 6.51 us -> none
    pallas_call x1, Pallas kernels: 53 us -> 49 us  [per_device(): pl.pallas_call(functools.partial(body, cfg), out_shape=(jax.ShapeDtypeStr...]
    reshape x2 -> x0, local copies, waits for them, and re-layouts: 2.57 us -> none  [per_device(): row = lambda x: x.reshape(1, -1)]
where the time goes in v2:
time: 115 us; the launch traced here: 114 us
  Pallas kernels  114 us (99%)
    pallas_call x1, Pallas kernels, per_device(): pl.pallas_call(hand_out, out_shape=tuple((jax.ShapeDtypeStruct(x.shape, x...  64.7 us
    pallas_call x1, Pallas kernels, per_device(): pl.pallas_call(functools.partial(body, cfg), out_shape=(jax.ShapeDtypeStr...  49 us

profile of v2, /device:TPU:25, one launch (start us, length us, event | category | flops | bytes accessed | tf_op | source)
XLA Modules:
  0.0 114.4 jit_solution(5370420428075993483)
XLA Ops:
  0.6 49.0 %shard_map.176 = (bf16[256,2048]{1,0:T(8,128)(2,1)}, bf16[256,2048]{1,0:T(8,128)(2,1)}) custom-call(bf16[256,1024]{1,0:T(8,128)(2,1)} %q_hbm.1, bf16[256,256]{1,0:T(8,128)(2,1)} %k_hbm.1, bf16[256,256]{1,0:T(8,128)(2,1)} %v_hbm.1, s32[1,1024]{1,0:T(1,128)} %bitcast.8, bf16[256,2048]{1,0:T(8,128)(2,1)} %hid_hbm.1, bf16[1024,2048]{1,0:T(8,128)(2,1)} %wo_hbm.1, ...), custom_call_target="tpu_custom_call" | custom-call | tf_op jit(solution)/shard_map/pallas_call | solution.py:531
  49.7 64.7 %shard_map.177 = (bf16[256,2048]{1,0:T(8,128)(2,1)}, bf16[256,2048]{1,0:T(8,128)(2,1)}) custom-call(bf16[256,2048]{1,0:T(8,128)(2,1)} %get-tuple-element.4.res_in, bf16[256,2048]{1,0:T(8,128)(2,1)} %get-tuple-element.5.mix_in), custom_call_target="tpu_custom_call" | custom-call | tf_op jit(solution)/shard_map/pallas_call | solution.py:548

commit v3 on v2

--- a/solution.py
+++ b/solution.py
@@ -18,6 +18,7 @@
 HALO = 16
 PAD = 8
 PIECES = 4
+CHUNK = 512
 LOW = -1e30
 F32 = jnp.float32
 BF16 = jnp.bfloat16
@@ -63,7 +64,9 @@
     PH = DI // SH
     heads = q.shape[1] // HEAD_DIM
     groups = ATT_HEADS // KV_HEADS
-    NC, _, W = carry_in.shape
+    NP, _, S = carry_in.shape
+    W = min(CHUNK, DI, D)
+    NC, cut = DI // W, W // S
     i = lax.axis_index("context")
     core = lax.axis_index("tensor")
     has_next = i + 1 < C
@@ -246,7 +249,7 @@
         part[:, at] = dot(att[core], wo[core, :, at])
         return carry
 
-    lax.fori_loop(0, D // W, project_own, 0)
+    lax.fori_loop(0, D // W, project_own, 0, unroll=2)
     locals_[4].wait()
     for copy in wcopies:
         copy.wait()
@@ -263,7 +266,7 @@
         r = r.astype(F32)
         return squares + jnp.sum(r * r, axis=1, keepdims=True)
 
-    squares = lax.fori_loop(0, D // W, project, jnp.zeros((T, 1), F32))
+    squares = lax.fori_loop(0, D // W, project, jnp.zeros((T, 1), F32), unroll=2)
     res_copy = pltpu.make_async_copy(res, res_hbm, local_sem.at[8])
     res_copy.start()
     inv = lax.rsqrt(squares / D + EPSILON)
@@ -288,7 +291,7 @@
         halo_out[:, at] = y[T - HALO :, :]
         return carry
 
-    lax.fori_loop(0, NC, project_inner, 0)
+    lax.fori_loop(0, NC, project_inner, 0, unroll=2)
     halo = remote(halo_out, halo_in, hsend.at[0], hrecv.at[0], context=i + 1)
 
     @pl.when(has_next)
@@ -310,15 +313,6 @@
     runT[...] = running.T
     stepT[...] = step[...].T
 
-    locals_[7].wait()
-
-    def project_gate(c, carry):
-        at = pl.ds(pl.multiple_of(c * W, LANES), W)
-        gated[:, at] = silu(dot(normed[...], wg[:, at]).astype(BF16).astype(F32))
-        return carry
-
-    lax.fori_loop(0, NC, project_gate, 0)
-
     @pl.when(has_prev)
     def _():
         halo.wait_recv()
@@ -363,29 +357,33 @@
     end = pieces(jnp.broadcast_to(end, (HALO, LANES)))
     cross = pm[B:, :B].astype(BF16)
 
+    def onward(p):
+        return remote(carry_out.at[p], carry_in.at[p], csend.at[p], crecv.at[p], context=i + 1)
+
     def convolve(c, carry):
         at = pl.ds(pl.multiple_of(c * W, LANES), W)
         value = conv(raw, ci_ref, at, W).astype(BF16)
         inner[:, at] = value
         weighted = (dot(coef[:T, :], pick[c]) * value.astype(F32)).astype(BF16)
-        state[c] = dot(rinT[...], weighted)
+        fresh = dot(rinT[...], weighted)
+        for k in range(cut):
+            state[c * cut + k] = fresh[:, k * S : (k + 1) * S]
+
+        @pl.when(has_next & jnp.logical_not(has_prev))
+        def _():
+            for k in range(cut):
+                carry_out[c * cut + k] = fresh[:, k * S : (k + 1) * S].astype(BF16)
+                onward(c * cut + k).start()
+
         return carry
 
     lax.fori_loop(0, NC, convolve, 0)
 
-    def onward(c):
-        return remote(carry_out.at[c], carry_in.at[c], csend.at[c], crecv.at[c], context=i + 1)
-
     @pl.when(jnp.logical_not(has_prev))
     def _():
         carry_in[...] = jnp.zeros(carry_in.shape, BF16)
 
-        @pl.when(has_next)
-        def _():
-            for c in range(NC):
-                carry_out[c] = state[c].astype(BF16)
-                onward(c).start()
-
+    locals_[7].wait()
     lane = lax.broadcasted_iota(jnp.int32, (T, LANES), 1)
     per = LANES // PH
 
@@ -411,24 +409,32 @@
             )
 
     def chunk(c, squares):
+        at = pl.ds(pl.multiple_of(c * W, LANES), W)
+
+        @pl.when(has_prev & has_next)
+        def _():
+            keeps = dot(end, pick[c])[:1, :]
+            for k in range(cut):
+                p = c * cut + k
+                onward(p).wait_recv()
+                moved = keeps[:, k * S : (k + 1) * S] * carry_in[p].astype(F32) + state[p]
+                carry_out[p] = moved.astype(BF16)
+                onward(p).start()
+
+        gated[:, at] = silu(dot(normed[...], wg[:, at]).astype(BF16).astype(F32))
         for n in range(W // LANES):
             pair(c * (W // LANES) + n)
-        at = pl.ds(pl.multiple_of(c * W, LANES), W)
-
-        @pl.when(has_prev)
+
+        @pl.when(has_prev & jnp.logical_not(has_next))
         def _():
-            onward(c).wait_recv()
-
-            @pl.when(has_next)
-            def _():
-                moved = dot(end, pick[c])[:1, :] * carry_in[c].astype(F32) + state[c]
-                carry_out[c] = moved.astype(BF16)
-                onward(c).start()
-
+            for k in range(cut):
+                onward(c * cut + k).wait_recv()
+
+        arrived = jnp.concatenate([carry_in[c * cut + k] for k in range(cut)], axis=1)
         early = (dot(coef[2 * T : 2 * T + B, :], pick[c]) * inner[:B, at].astype(F32)).astype(BF16)
         later = dot(cross, early) * dot(coef[2 * T + B :, :], pick[c])
         within[B:, at] = within[B:, at] + later
-        y = within[:, at] + dot(rout[...], carry_in[c]) * dot(coef[T : 2 * T, :], pick[c])
+        y = within[:, at] + dot(rout[...], arrived) * dot(coef[T : 2 * T, :], pick[c])
         y = y + skip[c, :1, :] * inner[:, at].astype(F32)
         y = y * gated[:, at]
         gated[:, at] = y
@@ -461,8 +467,8 @@
     @pl.when(has_next)
     def _():
         halo.wait_send()
-        for c in range(NC):
-            onward(c).wait_send()
+        for p in range(NP):
+            onward(p).wait_send()
         for d in range(reach):
             @pl.when(i >= d)
             def _():
@@ -473,16 +479,26 @@
     mix_copy.wait()
 
 
-def hand_out(res_in, mix_in, res_out, mix_out, sems):
-    copies = []
-    for n, (src, dst) in enumerate(((res_in, res_out), (mix_in, mix_out))):
+def hand_out(res_in, mix_in, res_out, mix_out, res_held, mix_held, sems):
+    inward, outward = [], []
+    for n, (src, held, dst) in enumerate(
+        ((res_in, res_held, res_out), (mix_in, mix_held, mix_out))
+    ):
         size = src.shape[0] // PIECES
         for k in range(PIECES):
             at = pl.ds(k * size, size)
-            copies.append(pltpu.make_async_copy(src.at[at], dst.at[at], sems.at[n * PIECES + k]))
-    for copy in copies:
+            inward.append(
+                pltpu.make_async_copy(src.at[at], held.at[at], sems.at[0, n * PIECES + k])
+            )
+            outward.append(
+                pltpu.make_async_copy(held.at[at], dst.at[at], sems.at[1, n * PIECES + k])
+            )
+    for copy in inward:
         copy.start()
-    for copy in copies:
+    for first, second in zip(inward, outward):
+        first.wait()
+        second.start()
+    for copy in outward:
         copy.wait()
 
 
@@ -498,8 +514,10 @@
     reach = min(-(-(WINDOW - 1) // T), C - 1)
     cfg = dict(cfg, reach=reach)
     heads = queries.shape[1] // HEAD_DIM
-    W = min(512, DI, D)
+    W = min(CHUNK, DI, D)
     NC = DI // W
+    S = min(W, 2 * LANES)
+    NP = DI // S
     hbm = pl.BlockSpec(memory_space=pl.ANY)
     vmem = pl.BlockSpec(memory_space=pltpu.VMEM)
     hops = max(reach, 1)
@@ -517,14 +535,14 @@
         V((HALO, DI + SN), BF16), V((PAD + T, LANES), F32), V((CONV - 1, T, LANES), F32),
         V((T, LANES), F32), V((T, LANES), F32), V((LANES, T), F32), V((LANES, T), F32),
         V((T, DI), BF16), V((T, STATE), BF16), V((STATE, T), BF16),
-        V((T, STATE), BF16), V((T, T), F32), V((NC, STATE, W), F32), V((NC, STATE, W), BF16),
-        V((NC, STATE, W), BF16), V((T, DI), F32), V((T, DI), F32), V((T, LANES), F32),
+        V((T, STATE), BF16), V((T, T), F32), V((NP, STATE, S), F32), V((NP, STATE, S), BF16),
+        V((NP, STATE, S), BF16), V((T, DI), F32), V((T, DI), F32), V((T, LANES), F32),
         V((peers, T, LANES), F32), V((T, D), F32), V((NC, 2 * LANES, W), BF16),
         V((3 * T, 2 * LANES), BF16), V((D // LANES, LANES), F32), V((DI // LANES, LANES), F32),
         V((NC, HALO, W), F32),
         dma((10,)), dma((hops,)), dma((hops,)), dma((hops,)), dma((hops,)),
         dma((peers,)), dma((peers,)), dma((peers,)), dma((peers,)), dma((1,)), dma((1,)),
-        dma((NC,)), dma((NC,)), dma((peers,)), dma((peers,)),
+        dma((NP,)), dma((NP,)), dma((peers,)), dma((peers,)),
     ]
     row = lambda x: x.reshape(1, -1)
     lanes = lambda x: x.reshape(-1, LANES)
@@ -550,7 +568,7 @@
         out_shape=tuple(jax.ShapeDtypeStruct(x.shape, x.dtype) for x in results),
         in_specs=[hbm, hbm],
         out_specs=(hbm, hbm),
-        scratch_shapes=[dma((2 * PIECES,))],
+        scratch_shapes=[V((T, D), BF16), V((T, DI), BF16), dma((2, 2 * PIECES))],
         compiler_params=pltpu.CompilerParams(vmem_limit_bytes=60 * 1024 * 1024),
     )(*results)
 

time: 115 us -> 48 us (0.42)
  Pallas kernels: 114 us -> 47.2 us
    pallas_call x1, Pallas kernels: 64.7 us -> 2.4 us  [per_device(): pl.pallas_call(hand_out, out_shape=tuple((jax.ShapeDtypeStruct(x.shape, x...]
    pallas_call x1, Pallas kernels: 49 us -> 44.8 us  [per_device(): pl.pallas_call(functools.partial(body, cfg), out_shape=(jax.ShapeDtypeStr...]
where the time goes in v3:
time: 48 us; the launch traced here: 47.9 us
  Pallas kernels  47.2 us (98%)
  between operations  0.65 us (1%)
    pallas_call x1, Pallas kernels, per_device(): pl.pallas_call(functools.partial(body, cfg), out_shape=(jax.ShapeDtypeStr...  44.8 us
    pallas_call x1, Pallas kernels, per_device(): pl.pallas_call(hand_out, out_shape=tuple((jax.ShapeDtypeStruct(x.shape, x...  2.4 us

profile of v3, /device:TPU:25, one launch (start us, length us, event | category | flops | bytes accessed | tf_op | source)
XLA Modules:
  0.0 47.9 jit_solution(8659761218230990542)
XLA Ops:
  0.6 44.8 %shard_map.176 = (bf16[256,2048]{1,0:T(8,128)(2,1)}, bf16[256,2048]{1,0:T(8,128)(2,1)}) custom-call(bf16[256,1024]{1,0:T(8,128)(2,1)} %q_hbm.1, bf16[256,256]{1,0:T(8,128)(2,1)} %k_hbm.1, bf16[256,256]{1,0:T(8,128)(2,1)} %v_hbm.1, s32[1,1024]{1,0:T(1,128)} %bitcast.8, bf16[256,2048]{1,0:T(8,128)(2,1)} %hid_hbm.1, bf16[1024,2048]{1,0:T(8,128)(2,1)} %wo_hbm.1, ...), custom_call_target="tpu_custom_call" | custom-call | tf_op jit(solution)/shard_map/pallas_call | solution.py:549
  45.5 2.4 %shard_map.177 = (bf16[256,2048]{1,0:T(8,128)(2,1)}, bf16[256,2048]{1,0:T(8,128)(2,1)}) custom-call(bf16[256,2048]{1,0:T(8,128)(2,1)} %get-tuple-element.4.res_in, bf16[256,2048]{1,0:T(8,128)(2,1)} %get-tuple-element.5.mix_in), custom_call_target="tpu_custom_call" | custom-call | tf_op jit(solution)/shard_map/pallas_call | solution.py:566

commit v4 on v3

--- a/solution.py
+++ b/solution.py
@@ -111,11 +111,27 @@
         barrier, has_next.astype(jnp.int32) + has_prev.astype(jnp.int32) + TP - 1
     )
 
-    def hop(d):
+    wcopies = [
+        remote(wo_hbm, wo.at[core], wsend.at[n], wrecv.at[n], tensor=partner)
+        for n, partner in enumerate(partners)
+    ]
+    for copy in wcopies:
+        copy.start()
+
+    kv_heads = kbuf.shape[2] // HEAD_DIM
+
+    def hop(d, g):
         to = i + 1
+        at = pl.ds(g * HEAD_DIM, HEAD_DIM)
         return (
-            remote(kbuf.at[d], kbuf.at[d + 1], ksend.at[d], krecv.at[d], context=to),
-            remote(vbuf.at[d], vbuf.at[d + 1], vsend.at[d], vrecv.at[d], context=to),
+            remote(
+                kbuf.at[d, :, at], kbuf.at[d + 1, :, at],
+                ksend.at[d, g], krecv.at[d, g], context=to,
+            ),
+            remote(
+                vbuf.at[d, :, at], vbuf.at[d + 1, :, at],
+                vsend.at[d, g], vrecv.at[d, g], context=to,
+            ),
         )
 
     locals_[1].wait()
@@ -123,16 +139,11 @@
     if reach > 0:
         @pl.when(has_next)
         def _():
-            for copy in hop(0):
-                copy.start()
+            for g in range(kv_heads):
+                for copy in hop(0, g):
+                    copy.start()
 
     for copy in locals_[3:]:
-        copy.start()
-    wcopies = [
-        remote(wo_hbm, wo.at[core], wsend.at[n], wrecv.at[n], tensor=partner)
-        for n, partner in enumerate(partners)
-    ]
-    for copy in wcopies:
         copy.start()
 
     rows = lax.broadcasted_iota(jnp.int32, (T, T), 0)
@@ -184,17 +195,18 @@
     acc[...] = jnp.zeros(acc.shape, F32)
     scale = HEAD_DIM ** (-0.5)
 
-    def attend(d):
+    def allow(d):
         gap = d * T + rows - cols
-        key_row = seg_row(i - d)
-        allowed = (gap >= 0) & (gap < WINDOW) & (segc[PAD:, :1] == key_row)
+        allowed = (gap >= 0) & (gap < WINDOW) & (segc[PAD:, :1] == seg_row(i - d))
         mask[...] = jnp.where(allowed, 0.0, LOW)
+
+    def attend(d, g):
+        kat = pl.ds(g * HEAD_DIM, HEAD_DIM)
 
         def one(h, carry):
             at = pl.multiple_of(h * HEAD_DIM, HEAD_DIM)
-            kat = pl.multiple_of((h // groups) * HEAD_DIM, HEAD_DIM)
             s = lax.dot_general(
-                q[:, pl.ds(at, HEAD_DIM)], kbuf[d, :, pl.ds(kat, HEAD_DIM)],
+                q[:, pl.ds(at, HEAD_DIM)], kbuf[d, :, kat],
                 (((1,), (1,)), ((), ())), preferred_element_type=F32,
             )
             s = s * scale + mask[...]
@@ -204,27 +216,31 @@
             p = jnp.exp(s - wide(new, T))
             m_s[h] = new
             l_s[h] = l_s[h] * alpha + jnp.sum(p, axis=1, keepdims=True)
-            acc[h] = acc[h] * alpha + dot(p.astype(BF16), vbuf[d, :, pl.ds(kat, HEAD_DIM)])
+            acc[h] = acc[h] * alpha + dot(p.astype(BF16), vbuf[d, :, kat])
             return carry
 
-        lax.fori_loop(0, heads, one, 0, unroll=4)
+        lax.fori_loop(g * groups, (g + 1) * groups, one, 0, unroll=True)
 
     locals_[0].wait()
-    attend(0)
+    allow(0)
+    for g in range(kv_heads):
+        attend(0, g)
 
     if reach > 0:
         def arrive(d, carry):
             @pl.when(i >= d)
             def _():
-                for copy in hop(d - 1):
-                    copy.wait_recv()
-
-                @pl.when(has_next & (d < reach))
-                def _():
-                    for copy in hop(d):
-                        copy.start()
-
-                attend(d)
+                allow(d)
+                for g in range(kv_heads):
+                    for copy in hop(d - 1, g):
+                        copy.wait_recv()
+
+                    @pl.when(has_next & (d < reach))
+                    def _():
+                        for copy in hop(d, g):
+                            copy.start()
+
+                    attend(d, g)
 
             return carry
 
@@ -249,7 +265,7 @@
         part[:, at] = dot(att[core], wo[core, :, at])
         return carry
 
-    lax.fori_loop(0, D // W, project_own, 0, unroll=2)
+    lax.fori_loop(0, D // W, project_own, 0, unroll=True)
     locals_[4].wait()
     for copy in wcopies:
         copy.wait()
@@ -266,9 +282,11 @@
         r = r.astype(F32)
         return squares + jnp.sum(r * r, axis=1, keepdims=True)
 
-    squares = lax.fori_loop(0, D // W, project, jnp.zeros((T, 1), F32), unroll=2)
+    squares = lax.fori_loop(0, D // W, project, jnp.zeros((T, 1), F32), unroll=True)
     res_copy = pltpu.make_async_copy(res, res_hbm, local_sem.at[8])
     res_copy.start()
+    locals_[5].wait()
+    locals_[6].wait()
     inv = lax.rsqrt(squares / D + EPSILON)
 
     def norm(c, carry):
@@ -276,13 +294,11 @@
         normed[:, at] = (res[:, at].astype(F32) * inv * row_of(gains, c)).astype(BF16)
         return carry
 
-    lax.fori_loop(0, D // W, norm, 0)
-
-    locals_[5].wait()
+    lax.fori_loop(0, D // W, norm, 0, unroll=True)
+
     x = dot(normed[...], ws[...]).astype(BF16)
     sraw[PAD:, :] = x.astype(F32)
     halo_out[:, DI:] = x[T - HALO :, :]
-    locals_[6].wait()
 
     def project_inner(c, carry):
         at = pl.ds(pl.multiple_of(c * W, LANES), W)
@@ -291,13 +307,7 @@
         halo_out[:, at] = y[T - HALO :, :]
         return carry
 
-    lax.fori_loop(0, NC, project_inner, 0, unroll=2)
-    halo = remote(halo_out, halo_in, hsend.at[0], hrecv.at[0], context=i + 1)
-
-    @pl.when(has_next)
-    def _():
-        halo.start()
-
+    lax.fori_loop(0, NC, project_inner, 0, unroll=True)
     raw_step = lax.dot_general(
         normed[...], wt_ref[...], (((1,), (1,)), ((), ())), preferred_element_type=F32
     ) + bias_ref[...]
@@ -312,6 +322,11 @@
     run[...] = running
     runT[...] = running.T
     stepT[...] = step[...].T
+    halo = remote(halo_out, halo_in, hsend.at[0], hrecv.at[0], context=i + 1)
+
+    @pl.when(has_next)
+    def _():
+        halo.start()
 
     @pl.when(has_prev)
     def _():
@@ -472,8 +487,9 @@
         for d in range(reach):
             @pl.when(i >= d)
             def _():
-                for copy in hop(d):
-                    copy.wait_send()
+                for g in range(kv_heads):
+                    for copy in hop(d, g):
+                        copy.wait_send()
 
     res_copy.wait()
     mix_copy.wait()
@@ -540,7 +556,8 @@
         V((peers, T, LANES), F32), V((T, D), F32), V((NC, 2 * LANES, W), BF16),
         V((3 * T, 2 * LANES), BF16), V((D // LANES, LANES), F32), V((DI // LANES, LANES), F32),
         V((NC, HALO, W), F32),
-        dma((10,)), dma((hops,)), dma((hops,)), dma((hops,)), dma((hops,)),
+        dma((10,)), dma((hops, KW // HEAD_DIM)), dma((hops, KW // HEAD_DIM)),
+        dma((hops, KW // HEAD_DIM)), dma((hops, KW // HEAD_DIM)),
         dma((peers,)), dma((peers,)), dma((peers,)), dma((peers,)), dma((1,)), dma((1,)),
         dma((NP,)), dma((NP,)), dma((peers,)), dma((peers,)),
     ]

time: 48 us -> 45.3 us (0.944)
  Pallas kernels: 47.2 us -> 44.5 us
    pallas_call x1, Pallas kernels: 44.8 us -> 42.1 us  [per_device(): pl.pallas_call(functools.partial(body, cfg), out_shape=(jax.ShapeDtypeStr...]
where the time goes in v4:
time: 45.3 us; the launch traced here: 45.2 us
  Pallas kernels  44.5 us (98%)
  between operations  0.65 us (1%)
    pallas_call x1, Pallas kernels, per_device(): pl.pallas_call(functools.partial(body, cfg), out_shape=(jax.ShapeDtypeStr...  42.1 us
    pallas_call x1, Pallas kernels, per_device(): pl.pallas_call(hand_out, out_shape=tuple((jax.ShapeDtypeStruct(x.shape, x...  2.4 us

profile of v4, /device:TPU:25, one launch (start us, length us, event | category | flops | bytes accessed | tf_op | source)
XLA Modules:
  0.0 45.2 jit_solution(1353065946954831577)
XLA Ops:
  0.6 42.1 %shard_map.176 = (bf16[256,2048]{1,0:T(8,128)(2,1)}, bf16[256,2048]{1,0:T(8,128)(2,1)}) custom-call(bf16[256,1024]{1,0:T(8,128)(2,1)} %q_hbm.1, bf16[256,256]{1,0:T(8,128)(2,1)} %k_hbm.1, bf16[256,256]{1,0:T(8,128)(2,1)} %v_hbm.1, s32[1,1024]{1,0:T(1,128)} %bitcast.8, bf16[256,2048]{1,0:T(8,128)(2,1)} %hid_hbm.1, bf16[1024,2048]{1,0:T(8,128)(2,1)} %wo_hbm.1, ...), custom_call_target="tpu_custom_call" | custom-call | tf_op jit(solution)/shard_map/pallas_call | solution.py:566
  42.8 2.4 %shard_map.177 = (bf16[256,2048]{1,0:T(8,128)(2,1)}, bf16[256,2048]{1,0:T(8,128)(2,1)}) custom-call(bf16[256,2048]{1,0:T(8,128)(2,1)} %get-tuple-element.4.res_in, bf16[256,2048]{1,0:T(8,128)(2,1)} %get-tuple-element.5.mix_in), custom_call_target="tpu_custom_call" | custom-call | tf_op jit(solution)/shard_map/pallas_call | solution.py:583

commit v5 on v4

--- a/solution.py
+++ b/solution.py
@@ -48,14 +48,15 @@
 
 def body(
     cfg,
-    q_hbm, k_hbm, v_hbm, seg_ref, hid_hbm, wo_hbm, gain_ref, wg_hbm, wi_hbm, ws_hbm, wt_ref,
-    ci_ref, cs_ref, bias_ref, decay_ref, skip_ref, og_ref,
+    q_hbm, k_hbm, v_hbm, seg_hbm, hid_hbm, wo_hbm, gain_hbm, wg_hbm, wi_hbm, ws_hbm, wt_hbm,
+    ci_hbm, cs_hbm, bias_hbm, decay_hbm, skip_hbm, og_hbm,
     res_hbm, mix_hbm,
     q, kbuf, vbuf, hid, wo, wg, wi, ws, att, m_s, l_s, acc, mask, res, normed,
     raw, sraw, halo_out, halo_in, segc, keep, step, run, runT, stepT, inner, rin, rinT, rout,
     pm, state, carry_in, carry_out, within, gated, sq, sq_in, part, pick, coef, gains, og, skip,
     local_sem, ksend, krecv, vsend, vrecv, wsend, wrecv, asend, arecv, hsend, hrecv,
     csend, crecv, ssend, srecv,
+    seg_ref, gain_ref, wt_ref, ci_ref, cs_ref, bias_ref, decay_ref, skip_ref, og_ref, small_sem,
 ):
     C, TP, reach = cfg["context"], cfg["tensor"], cfg["reach"]
     T, D = hid.shape
@@ -104,8 +105,14 @@
              (hid_hbm, hid), (ws_hbm, ws), (wi_hbm, wi), (wg_hbm, wg)]
         )
     ]
-    for copy in locals_[:3]:
-        copy.start()
+    small = [
+        pltpu.make_async_copy(src, dst, small_sem.at[n])
+        for n, (src, dst) in enumerate(
+            [(seg_hbm, seg_ref), (gain_hbm, gain_ref), (og_hbm, og_ref), (skip_hbm, skip_ref),
+             (wt_hbm, wt_ref), (ci_hbm, ci_ref), (cs_hbm, cs_ref), (bias_hbm, bias_ref),
+             (decay_hbm, decay_ref)]
+        )
+    ]
 
     pl.semaphore_wait(
         barrier, has_next.astype(jnp.int32) + has_prev.astype(jnp.int32) + TP - 1
@@ -115,27 +122,23 @@
         remote(wo_hbm, wo.at[core], wsend.at[n], wrecv.at[n], tensor=partner)
         for n, partner in enumerate(partners)
     ]
-    for copy in wcopies:
-        copy.start()
-
     kv_heads = kbuf.shape[2] // HEAD_DIM
 
     def hop(d, g):
         to = i + 1
         at = pl.ds(g * HEAD_DIM, HEAD_DIM)
+        first = isinstance(d, int) and d == 0
         return (
             remote(
-                kbuf.at[d, :, at], kbuf.at[d + 1, :, at],
+                k_hbm.at[:, at] if first else kbuf.at[d, :, at], kbuf.at[d + 1, :, at],
                 ksend.at[d, g], krecv.at[d, g], context=to,
             ),
             remote(
-                vbuf.at[d, :, at], vbuf.at[d + 1, :, at],
+                v_hbm.at[:, at] if first else vbuf.at[d, :, at], vbuf.at[d + 1, :, at],
                 vsend.at[d, g], vrecv.at[d, g], context=to,
             ),
         )
 
-    locals_[1].wait()
-    locals_[2].wait()
     if reach > 0:
         @pl.when(has_next)
         def _():
@@ -143,8 +146,10 @@
                 for copy in hop(0, g):
                     copy.start()
 
-    for copy in locals_[3:]:
+    for copy in small[:4] + locals_[:3] + wcopies + locals_[3:] + small[4:]:
         copy.start()
+    for copy in small[:4]:
+        copy.wait()
 
     rows = lax.broadcasted_iota(jnp.int32, (T, T), 0)
     cols = lax.broadcasted_iota(jnp.int32, (T, T), 1)
@@ -221,7 +226,8 @@
 
         lax.fori_loop(g * groups, (g + 1) * groups, one, 0, unroll=True)
 
-    locals_[0].wait()
+    for copy in locals_[:3]:
+        copy.wait()
     allow(0)
     for g in range(kv_heads):
         attend(0, g)
@@ -287,6 +293,8 @@
     res_copy.start()
     locals_[5].wait()
     locals_[6].wait()
+    for copy in small[4:]:
+        copy.wait()
     inv = lax.rsqrt(squares / D + EPSILON)
 
     def norm(c, carry):
@@ -470,14 +478,14 @@
         grand = grand + sq_in[n]
     factor = wide(lax.rsqrt(grand / (DI * TP) + EPSILON), W)
 
-    def scale_out(c, carry):
-        at = pl.ds(pl.multiple_of(c * W, LANES), W)
+    mix_copies = []
+    for c in range(NC):
+        at = pl.ds(c * W, W)
         inner[:, at] = (gated[:, at] * factor * row_of(og, c)).astype(BF16)
-        return carry
-
-    lax.fori_loop(0, NC, scale_out, 0)
-    mix_copy = pltpu.make_async_copy(inner, mix_hbm, local_sem.at[9])
-    mix_copy.start()
+        mix_copies.append(
+            pltpu.make_async_copy(inner.at[:, at], mix_hbm.at[:, at], local_sem.at[9 + c])
+        )
+        mix_copies[-1].start()
 
     @pl.when(has_next)
     def _():
@@ -492,7 +500,8 @@
                         copy.wait_send()
 
     res_copy.wait()
-    mix_copy.wait()
+    for copy in mix_copies:
+        copy.wait()
 
 
 def hand_out(res_in, mix_in, res_out, mix_out, res_held, mix_held, sems):
@@ -535,7 +544,6 @@
     S = min(W, 2 * LANES)
     NP = DI // S
     hbm = pl.BlockSpec(memory_space=pl.ANY)
-    vmem = pl.BlockSpec(memory_space=pltpu.VMEM)
     hops = max(reach, 1)
     peers = max(TP - 1, 1)
     V = pltpu.VMEM
@@ -556,20 +564,25 @@
         V((peers, T, LANES), F32), V((T, D), F32), V((NC, 2 * LANES, W), BF16),
         V((3 * T, 2 * LANES), BF16), V((D // LANES, LANES), F32), V((DI // LANES, LANES), F32),
         V((NC, HALO, W), F32),
-        dma((10,)), dma((hops, KW // HEAD_DIM)), dma((hops, KW // HEAD_DIM)),
+        dma((9 + NC,)), dma((hops, KW // HEAD_DIM)), dma((hops, KW // HEAD_DIM)),
         dma((hops, KW // HEAD_DIM)), dma((hops, KW // HEAD_DIM)),
         dma((peers,)), dma((peers,)), dma((peers,)), dma((peers,)), dma((1,)), dma((1,)),
         dma((NP,)), dma((NP,)), dma((peers,)), dma((peers,)),
     ]
     row = lambda x: x.reshape(1, -1)
     lanes = lambda x: x.reshape(-1, LANES)
+    small = [
+        row(segment_ids), lanes(norm_gain), step_weight.T, conv_inner, conv_state,
+        row(step_bias), row(decay_log), row(skip_gain), lanes(out_gain),
+    ]
+    scratch += [V(x.shape, x.dtype) for x in small] + [dma((len(small),))]
     results = pl.pallas_call(
         functools.partial(body, cfg),
         out_shape=(
             jax.ShapeDtypeStruct((T, D), BF16),
             jax.ShapeDtypeStruct((T, DI), BF16),
         ),
-        in_specs=[hbm, hbm, hbm, vmem, hbm, hbm, vmem, hbm, hbm, hbm] + [vmem] * 7,
+        in_specs=[hbm] * 17,
         out_specs=(hbm, hbm),
         scratch_shapes=scratch,
         compiler_params=pltpu.CompilerParams(

time: 45.3 us -> 44.6 us (0.985)
  Pallas kernels: 44.5 us -> 43.8 us
    pallas_call x1, Pallas kernels: 42.1 us -> 41.4 us  [per_device(): pl.pallas_call(functools.partial(body, cfg), out_shape=(jax.ShapeDtypeStr...]
where the time goes in v5:
time: 44.6 us; the launch traced here: 44.4 us
  Pallas kernels  43.8 us (98%)
  between operations  0.65 us (1%)
    pallas_call x1, Pallas kernels, per_device(): pl.pallas_call(functools.partial(body, cfg), out_shape=(jax.ShapeDtypeStr...  41.4 us
    pallas_call x1, Pallas kernels, per_device(): pl.pallas_call(hand_out, out_shape=tuple((jax.ShapeDtypeStruct(x.shape, x...  2.4 us

profile of v5, /device:TPU:25, one launch (start us, length us, event | category | flops | bytes accessed | tf_op | source)
XLA Modules:
  0.0 44.4 jit_solution(1331433561387501914)
XLA Ops:
  0.6 41.4 %shard_map.176 = (bf16[256,2048]{1,0:T(8,128)(2,1)}, bf16[256,2048]{1,0:T(8,128)(2,1)}) custom-call(bf16[256,1024]{1,0:T(8,128)(2,1)} %q_hbm.1, bf16[256,256]{1,0:T(8,128)(2,1)} %k_hbm.1, bf16[256,256]{1,0:T(8,128)(2,1)} %v_hbm.1, s32[1,1024]{1,0:T(1,128)} %bitcast.8, bf16[256,2048]{1,0:T(8,128)(2,1)} %hid_hbm.1, bf16[1024,2048]{1,0:T(8,128)(2,1)} %wo_hbm.1, ...), custom_call_target="tpu_custom_call" | custom-call | tf_op jit(solution)/shard_map/pallas_call | solution.py:579
  42.0 2.4 %shard_map.177 = (bf16[256,2048]{1,0:T(8,128)(2,1)}, bf16[256,2048]{1,0:T(8,128)(2,1)}) custom-call(bf16[256,2048]{1,0:T(8,128)(2,1)} %get-tuple-element.4.res_in, bf16[256,2048]{1,0:T(8,128)(2,1)} %get-tuple-element.5.mix_in), custom_call_target="tpu_custom_call" | custom-call | tf_op jit(solution)/shard_map/pallas_call | solution.py:596
